TPU v7x, 32 devices: a whole 2x2x4 slice. The times are simulated.
32 devices in a mesh: expert: 16 (over z, y, x), tensor: 2 (over core).
Axes of the slice: x: 2, y: 2, z: 4, core: 2. Of those that a mesh axis runs over, the one named last changes fastest.
Arguments:
- tokens: bfloat16 [768, 4096], P('expert', 'tensor'), may hold values from -6 to 6
- cotangent: bfloat16 [768, 4096], P('expert', 'tensor'), may hold values from -6 to 6
- expert_ids: int32 [768, 8], P('expert'), may hold values from 0 to 15, all different within a row; in each aligned block of 48 rows (0 to 47, 48 to 95, ...) at most 32 rows name the same one
- gate_values: float32 [768, 8], P('expert'), may hold values from 0.05 to 1
- w_gate: bfloat16 [16, 768, 4096], P('expert', 'tensor'), may hold values from -0.09375 to 0.09375
- w_up: bfloat16 [16, 768, 4096], P('expert', 'tensor'), may hold values from -0.09375 to 0.09375
- w_down: bfloat16 [16, 768, 4096], P('expert', 'tensor'), may hold values from -0.21875 to 0.21875
Outputs:
- grad_tokens: bfloat16 [768, 4096], P('expert', 'tensor')
- grad_gate: bfloat16 [16, 768, 4096], P('expert', 'tensor')
- grad_up: bfloat16 [16, 768, 4096], P('expert', 'tensor')
- grad_down: bfloat16 [16, 768, 4096], P('expert', 'tensor')
Inputs may be any that keep to these rules, and one draw needn't show every extreme that they name: `expert_ids`: each row names 8 different experts. Among the 48 tokens of one index of the expert axis no expert is named more than 32 times, and in every draw some expert is named exactly 32 times there.
All inputs are finite; a program needn't handle non-finite values.
Results may differ from a plain program's by a relative error of at most 0.019.
Values may be sent and summed in bfloat16 or wider, within the bound.
A program may use at most 64 MiB of HBM per device.

v0:
```python
import jax
import jax.numpy as jnp
from jax import lax
from jax.sharding import PartitionSpec as P

TOP = 8


def expert_backward(rows_x, rows_d, w_gate, w_up, w_down):
    gate_pre = jnp.einsum("secd,ehd->sech", rows_x, w_gate, preferred_element_type=jnp.float32)
    up_pre = jnp.einsum("secd,ehd->sech", rows_x, w_up, preferred_element_type=jnp.float32)
    sigmoid = jax.nn.sigmoid(gate_pre)
    active = gate_pre * sigmoid
    hidden = (active * up_pre).astype(jnp.bfloat16)
    hidden_grad = jnp.einsum("secd,ehd->sech", rows_d, w_down, preferred_element_type=jnp.float32)
    up_grad = (hidden_grad * active).astype(jnp.bfloat16)
    gate_grad = (hidden_grad * up_pre * sigmoid * (1.0 + gate_pre * (1.0 - sigmoid))).astype(
        jnp.bfloat16
    )
    grad_gate = jnp.einsum(
        "sech,secd->ehd", gate_grad, rows_x, preferred_element_type=jnp.float32
    ).astype(jnp.bfloat16)
    grad_up = jnp.einsum(
        "sech,secd->ehd", up_grad, rows_x, preferred_element_type=jnp.float32
    ).astype(jnp.bfloat16)
    grad_down = jnp.einsum(
        "sech,secd->ehd", hidden, rows_d, preferred_element_type=jnp.float32
    ).astype(jnp.bfloat16)
    partial_value = jnp.einsum(
        "sech,ehd->secd", gate_grad, w_gate, preferred_element_type=jnp.float32
    )
    partial_value = partial_value + jnp.einsum(
        "sech,ehd->secd", up_grad, w_up, preferred_element_type=jnp.float32
    )
    return (partial_value, grad_gate, grad_up, grad_down)


def on_device(tokens, cotangent, expert_ids, gate_values, w_gate, w_up, w_down):
    tok_count = expert_ids.shape[0]
    local_count = w_gate.shape[0]
    groups = lax.axis_size("expert")
    experts = local_count * groups
    capacity = 4 * tok_count * TOP // (3 * experts)
    feat_width = tokens.shape[1]
    flat_ids = expert_ids.reshape(-1)
    onehot = (flat_ids[:, None] == jnp.arange(experts, dtype=jnp.int32)[None, :]).astype(jnp.int32)
    before = jnp.cumsum(onehot, axis=0) - onehot
    slot_pos = jnp.sum(before * onehot, axis=1)
    target = flat_ids * capacity + slot_pos
    matches = (target[None, :] == jnp.arange(experts * capacity, dtype=jnp.int32)[:, None]).reshape(
        experts * capacity, tok_count, TOP
    )
    by_token = jnp.any(matches, axis=2)
    occupied = jnp.any(by_token, axis=1)
    token_iota = jnp.arange(tok_count, dtype=jnp.int32)
    owner = jnp.sum(jnp.where(by_token, token_iota[None, :], 0), axis=1)
    slot_weight = jnp.sum(jnp.sum(jnp.where(matches, gate_values[None, :, :], 0.0), axis=2), axis=1)
    full_x, full_d = (
        lax.all_gather(tokens, "tensor", axis=1, tiled=True),
        lax.all_gather(cotangent, "tensor", axis=1, tiled=True),
    )
    sent_x = jnp.where(occupied[:, None], full_x[owner], jnp.zeros((), jnp.bfloat16))
    sent_d = (slot_weight[:, None] * full_d[owner].astype(jnp.float32)).astype(jnp.bfloat16)
    buffer_shape = (groups, local_count, capacity, full_x.shape[1])
    sent_x, sent_d = (sent_x.reshape(buffer_shape), sent_d.reshape(buffer_shape))
    rows_x, rows_d = (
        lax.all_to_all(sent_x, "expert", split_axis=0, concat_axis=0, tiled=True),
        lax.all_to_all(sent_d, "expert", split_axis=0, concat_axis=0, tiled=True),
    )
    partial_value, grad_gate, grad_up, grad_down = expert_backward(
        rows_x, rows_d, w_gate, w_up, w_down
    )
    summed = lax.psum(partial_value.astype(jnp.bfloat16), "tensor").astype(jnp.float32)
    returned = lax.dynamic_slice_in_dim(
        summed, lax.axis_index("tensor") * feat_width, feat_width, 3
    ).astype(jnp.bfloat16)
    arrived = lax.all_to_all(returned, "expert", split_axis=0, concat_axis=0, tiled=True).reshape(
        experts * capacity, feat_width
    )
    masked = jnp.where(occupied[:, None], arrived.astype(jnp.float32), jnp.zeros((), jnp.float32))
    grad_tokens = jax.ops.segment_sum(masked, owner, num_segments=tok_count).astype(jnp.bfloat16)
    return (grad_tokens, grad_gate, grad_up, grad_down)


def solution(mesh):
    return jax.shard_map(
        on_device,
        mesh=mesh,
        in_specs=(
            P("expert", "tensor"),
            P("expert", "tensor"),
            P("expert", None),
            P("expert", None),
            P("expert", "tensor", None),
            P("expert", "tensor", None),
            P("expert", "tensor", None),
        ),
        out_specs=(
            P("expert", "tensor"),
            P("expert", "tensor", None),
            P("expert", "tensor", None),
            P("expert", "tensor", None),
        ),
        check_vma=False,
    )
```

profile of v0, /device:TPU:0, one launch (start us, length us, event | category | flops | bytes accessed | tf_op | source)
XLA Modules:
  0.0 334.2 jit_solution(10640285187974878907)
XLA Ops:
  7.2 0.9 copy.37
  11.2 2.4 all_gather.7
  13.6 4.3 %gather_fusion.1 = bf16[512,4096]{1,0:T(8,128)(2,1)} fusion(bf16[48,4096]{1,0:T(8,128)(2,1)S(1)} %all_gather.7, s32[1024]{0:T(1024)S(1)} %pad_clamp_fusion), kind=kCustom, calls=%fused_computation.1 | custom fusion | bytes 8390656 | tf_op jit(solution)/shard_map/gather | solution.py:62
  17.9 4.5 %broadcast_select_fusion = bf16[16,1,32,4096]{3,2,1,0:T(8,128)(2,1)} fusion(bf16[16,1,32,4096]{3,2,1,0:T(8,128)(2,1)} %bitcast.137, pred[16,32]{1,0:T(8,128)(4,1)S(1)} %broadcast_in_dim.73), kind=kLoop, calls=%fused_computation.25 | loop fusion | flops 2097152 | bytes 8389120 | tf_op jit(solution)/shard_map/jit(_where)/select_n | solution.py:62
  22.4 8.4 %all-to-all-start.1 = ((bf16[16,1,32,4096]{3,2,1,0:T(8,128)(2,1)}), bf16[16,1,32,4096]{3,2,1,0:T(8,128)(2,1)}, u32[]{:S(2)}, u32[]{:S(2)}) async-start(bf16[16,1,32,4096]{3,2,1,0:T(8,128)(2,1)} %broadcast_select_fusion), calls=%async_computation.1 | async-start | bytes 8388608 | tf_op jit(solution)/shard_map/all_to_all | solution.py:67
  31.2 2.3 all_gather.6
  33.5 4.4 %gather_fusion = bf16[512,4096]{1,0:T(8,128)(2,1)} fusion(bf16[48,4096]{1,0:T(8,128)(2,1)S(1)} %all_gather.6, s32[1024]{0:T(1024)S(1)} %pad_clamp_fusion), kind=kCustom, calls=%fused_computation | custom fusion | bytes 8390656 | tf_op jit(solution)/shard_map/gather | solution.py:63
  37.9 5.6 %fusion = bf16[16,1,32,4096]{3,2,1,0:T(8,128)(2,1)} fusion(bf16[16,1,32,4096]{3,2,1,0:T(8,128)(2,1)} %bitcast.136, f32[16,32]{1,0:T(8,128)S(1)} %mul.57), kind=kLoop, calls=%fused_computation.4 | loop fusion | flops 6291456 | bytes 8390656 | tf_op jit(solution)/shard_map/convert_element_type | solution.py:63
  43.5 67.7 %all-to-all-done.1 = bf16[16,1,32,4096]{3,2,1,0:T(8,128)(2,1)} async-done(((bf16[16,1,32,4096]{3,2,1,0:T(8,128)(2,1)}), bf16[16,1,32,4096]{3,2,1,0:T(8,128)(2,1)}, u32[]{:S(2)}, u32[]{:S(2)}) %all-to-all-start.1) | async-done | bytes 4194336 | tf_op jit(solution)/shard_map/all_to_all | solution.py:67
  111.2 20.3 %all-to-all-start = ((bf16[16,1,32,4096]{3,2,1,0:T(8,128)(2,1)}), bf16[16,1,32,4096]{3,2,1,0:T(8,128)(2,1)}, u32[]{:S(2)}, u32[]{:S(2)}) async-start(bf16[16,1,32,4096]{3,2,1,0:T(8,128)(2,1)} %fusion), calls=%async_computation | async-start | bytes 8388608 | tf_op jit(solution)/shard_map/all_to_all | solution.py:68
  131.7 5.6 %fusion.34 = f32[16,1,32,384]{3,2,0,1:T(8,128)} fusion(bf16[1,384,4096]{2,1,0:T(8,128)(2,1)S(1)} %copy-done, bf16[16,1,32,4096]{3,2,1,0:T(8,128)(2,1)} %all-to-all-done.1), kind=kOutput, calls=%fused_computation.37 | convolution fusion | flops 1610612736 | bytes 8126464 | tf_op jit(solution)/shard_map/secd,ehd->sech/dot_general | solution.py:10
  137.3 5.4 %fusion.29 = f32[16,1,32,384]{3,2,0,1:T(8,128)} fusion(bf16[1,384,4096]{2,1,0:T(8,128)(2,1)S(1)} %copy-done.1, bf16[16,1,32,4096]{3,2,1,0:T(8,128)(2,1)} %all-to-all-done.1), kind=kOutput, calls=%fused_computation.36 | convolution fusion | flops 1610612736 | bytes 8126464 | tf_op jit(solution)/shard_map/secd,ehd->sech/dot_general | solution.py:11
  142.7 67.3 %all-to-all-done = bf16[16,1,32,4096]{3,2,1,0:T(8,128)(2,1)} async-done(((bf16[16,1,32,4096]{3,2,1,0:T(8,128)(2,1)}), bf16[16,1,32,4096]{3,2,1,0:T(8,128)(2,1)}, u32[]{:S(2)}, u32[]{:S(2)}) %all-to-all-start) | async-done | bytes 4194336 | tf_op jit(solution)/shard_map/all_to_all | solution.py:68
  210.0 6.0 %fusion.42 = (bf16[16,32,384]{2,1,0:T(8,128)(2,1)S(1)}, bf16[16,1,32,384]{3,2,0,1:T(8,128)(2,1)S(1)}) fusion(f32[16,1,32,384]{3,2,0,1:T(8,128)} %fusion.34, f32[16,1,32,384]{3,2,0,1:T(8,128)} %fusion.29, bf16[1,384,4096]{2,1,0:T(8,128)(2,1)} %param.13, bf16[16,1,32,4096]{3,2,1,0:T(8,128)(2,1)} %all-to-all-done), kind=kOutput, calls=%fused_computation.47 | convolution fusion | flops 1613168640 | bytes 9699328 | tf_op jit(solution)/shard_map/secd,ehd->sech/dot_general | solution.py:15
  216.1 2.3 fusion.15
  218.4 4.3 %fusion.1 = bf16[16,1,32,4096]{3,2,0,1:T(8,128)(2,1)} fusion(f32[16,32,4096]{2,1,0:T(8,128)S(1)} %fusion.15, bf16[16,32,384]{2,1,0:T(8,128)(2,1)S(1)} %get-tuple-element.6, bf16[1,384,4096]{2,1,0:T(8,128)(2,1)S(1)} %copy-done.2), kind=kOutput, calls=%fused_computation.9 | convolution fusion | flops 1614807040 | bytes 16121856 | tf_op jit(solution)/shard_map/sech,ehd->secd/dot_general | solution.py:32
  222.8 42.3 %all-reduce.2.cloned.1.call-done = bf16[16,1,32,4096]{3,2,0,1:T(8,128)(2,1)} async-done(((bf16[16,1,32,4096]{3,2,0,1:T(8,128)(2,1)}), bf16[16,1,32,4096]{3,2,0,1:T(8,128)(2,1)}) %all-reduce.2.cloned.1.call-update) | async-done | bytes 4194320 | tf_op jit(solution)/shard_map/psum | solution.py:73
  265.1 3.2 fusion.21
  268.3 6.8 %all-to-all-start.2 = ((bf16[16,1,32,2048]{3,2,1,0:T(8,128)(2,1)}), bf16[16,1,32,2048]{3,2,1,0:T(8,128)(2,1)}, u32[]{:S(2)}, u32[]{:S(2)}) async-start(bf16[16,1,32,2048]{3,2,1,0:T(8,128)(2,1)} %fusion.21), calls=%async_computation.2 | async-start | bytes 4194304 | tf_op jit(solution)/shard_map/all_to_all | solution.py:77
  275.1 5.8 %fusion.3 = bf16[1,384,4096]{2,1,0:T(8,128)(2,1)} fusion(bf16[16,32,384]{2,1,0:T(8,128)(2,1)} %copy-done.3, bf16[16,1,32,4096]{3,2,1,0:T(8,128)(2,1)} %all-to-all-done.1), kind=kOutput, calls=%fused_computation.11 | convolution fusion | flops 1612185600 | bytes 7733248 | tf_op jit(solution)/shard_map/sech,secd->ehd/dot_general | solution.py:23
  280.9 5.8 %fusion.2 = bf16[1,384,4096]{2,1,0:T(8,128)(2,1)} fusion(bf16[16,1,32,4096]{3,2,1,0:T(8,128)(2,1)} %all-to-all-done.1, bf16[16,1,32,384]{3,2,0,1:T(8,128)(2,1)S(1)} %get-tuple-element.7), kind=kOutput, calls=%fused_computation.10 | convolution fusion | flops 1612185600 | bytes 7733248 | tf_op jit(solution)/shard_map/sech,secd->ehd/dot_general | solution.py:20
  286.7 5.7 %fusion.4 = bf16[1,384,4096]{2,1,0:T(8,128)(2,1)} fusion(bf16[16,1,32,4096]{3,2,1,0:T(8,128)(2,1)} %all-to-all-done, f32[16,1,32,384]{3,2,0,1:T(8,128)S(1)} %copy-done.5, f32[16,1,32,384]{3,2,0,1:T(8,128)S(1)} %copy-done.4), kind=kOutput, calls=%fused_computation.12 | convolution fusion | flops 1613365248 | bytes 8912896 | tf_op jit(solution)/shard_map/sech,secd->ehd/dot_general | solution.py:26
  292.5 25.9 %all-to-all-done.2 = bf16[16,1,32,2048]{3,2,1,0:T(8,128)(2,1)} async-done(((bf16[16,1,32,2048]{3,2,1,0:T(8,128)(2,1)}), bf16[16,1,32,2048]{3,2,1,0:T(8,128)(2,1)}, u32[]{:S(2)}, u32[]{:S(2)}) %all-to-all-start.2) | async-done | bytes 2097184 | tf_op jit(solution)/shard_map/all_to_all | solution.py:77
  318.4 8.3 %scatter_custom_fusion = f32[48,2048]{1,0:T(8,128)S(1)} fusion(s32[512]{0:T(512)S(1)} %select_reduce_fusion.1, bf16[512,2048]{1,0:T(8,128)(2,1)} %bitcast.49, f32[]{:T(128)} %constant.10.clone.1, pred[512]{0:T(512)(128)(4,1)S(1)} %copy-done.9), kind=kCustom, calls=%fused_computation.14 | custom fusion | flops 3145728 | bytes 2491904 | tf_op jit(solution)/shard_map/scatter-add | solution.py:81
  (44 shorter events, 4.3 us)
Async XLA Ops:
  7.2 124.6 %copy-start = (bf16[1,384,4096]{2,1,0:T(8,128)(2,1)S(1)}, bf16[1,384,4096]{2,1,0:T(8,128)(2,1)}, u32[]{:S(2)}) copy-start(bf16[1,384,4096]{2,1,0:T(8,128)(2,1)} %param.11) | copy-start | bytes 9437188
  10.5 0.6 copy-start.6
  10.8 7.1 %copy-start.8 = (pred[512]{0:T(512)(128)(4,1)}, pred[512]{0:T(512)(128)(4,1)S(1)}, u32[]{:S(2)}) copy-start(pred[512]{0:T(512)(128)(4,1)S(1)} %get-tuple-element.4) | copy-start | bytes 1540
  22.4 8.4 %copy-start.10 = (f32[48,8]{0,1:T(8,128)S(1)}, f32[48,8]{0,1:T(8,128)}, u32[]{:S(2)}) copy-start(f32[48,8]{0,1:T(8,128)} %param.10) | copy-start | bytes 4612
  22.4 8.5 %copy-start.7 = (s32[48,8]{1,0:T(8,128)S(1)}, s32[48,8]{1,0:T(8,128)}, u32[]{:S(2)}) copy-start(s32[48,8]{1,0:T(8,128)} %copy-done.6) | copy-start | bytes 4612
  22.4 88.8 %all-to-all-start.1 = ((bf16[16,1,32,4096]{3,2,1,0:T(8,128)(2,1)}), bf16[16,1,32,4096]{3,2,1,0:T(8,128)(2,1)}, u32[]{:S(2)}, u32[]{:S(2)}) async-start(bf16[16,1,32,4096]{3,2,1,0:T(8,128)(2,1)} %broadcast_select_fusion), calls=%async_computation.1 | async-start | bytes 8388608 | tf_op jit(solution)/shard_map/all_to_all | solution.py:67
  111.2 98.8 %all-to-all-start = ((bf16[16,1,32,4096]{3,2,1,0:T(8,128)(2,1)}), bf16[16,1,32,4096]{3,2,1,0:T(8,128)(2,1)}, u32[]{:S(2)}, u32[]{:S(2)}) async-start(bf16[16,1,32,4096]{3,2,1,0:T(8,128)(2,1)} %fusion), calls=%async_computation | async-start | bytes 8388608 | tf_op jit(solution)/shard_map/all_to_all | solution.py:68
  131.5 133.6 %all-reduce.2.cloned.1.call-start = ((), (), s32[]{:S(2)}) async-start(), calls=%async_computation.3 | async-start | bytes 8388608 | tf_op jit(solution)/shard_map/psum | solution.py:73
  131.7 5.6 %copy-start.1 = (bf16[1,384,4096]{2,1,0:T(8,128)(2,1)S(1)}, bf16[1,384,4096]{2,1,0:T(8,128)(2,1)}, u32[]{:S(2)}) copy-start(bf16[1,384,4096]{2,1,0:T(8,128)(2,1)} %param.12) | copy-start | bytes 9437188
  216.0 2.4 copy-start.3
  216.0 2.4 copy-start.2
  268.3 50.1 %all-to-all-start.2 = ((bf16[16,1,32,2048]{3,2,1,0:T(8,128)(2,1)}), bf16[16,1,32,2048]{3,2,1,0:T(8,128)(2,1)}, u32[]{:S(2)}, u32[]{:S(2)}) async-start(bf16[16,1,32,2048]{3,2,1,0:T(8,128)(2,1)} %fusion.21), calls=%async_computation.2 | async-start | bytes 4194304 | tf_op jit(solution)/shard_map/all_to_all | solution.py:77
  280.9 5.8 %copy-start.4 = (f32[16,1,32,384]{3,2,0,1:T(8,128)S(1)}, f32[16,1,32,384]{3,2,0,1:T(8,128)}, u32[]{:S(2)}) copy-start(f32[16,1,32,384]{3,2,0,1:T(8,128)} %fusion.34) | copy-start | bytes 2359300
  280.9 5.8 %copy-start.5 = (f32[16,1,32,384]{3,2,0,1:T(8,128)S(1)}, f32[16,1,32,384]{3,2,0,1:T(8,128)}, u32[]{:S(2)}) copy-start(f32[16,1,32,384]{3,2,0,1:T(8,128)} %fusion.29) | copy-start | bytes 2359300
  286.7 31.6 %copy-start.9 = (pred[512]{0:T(512)(128)(4,1)S(1)}, pred[512]{0:T(512)(128)(4,1)}, u32[]{:S(2)}) copy-start(pred[512]{0:T(512)(128)(4,1)} %copy-done.8) | copy-start | bytes 1540
Sparse Core Ops, SparseCore 0:
  222.9 42.1 all-reduce.1
where the time goes:
time: 339 us; the launch traced here: 334 us
  waiting for transfers between devices  203 us (60%)
  matrix products  41 us (12%)
  starting transfers between devices  35.7 us (11%)
  other arithmetic  24.6 us (7%)
  between operations  14.2 us (4%)
  local copies, waits for them, and re-layouts  10.8 us (3%)
  blocking collectives  4.71 us (1%)
    all_to_all x1, waiting for transfers between devices, on_device(): lax.all_to_all(sent_x, 'expert', split_axis=0, concat_axis=0, tiled=True)  67.7 us
    all_to_all x1, waiting for transfers between devices, on_device(): lax.all_to_all(sent_d, 'expert', split_axis=0, concat_axis=0, tiled=True)  67.3 us
    psum x1, waiting for transfers between devices, on_device(): lax.psum(partial_value.astype(jnp.bfloat16), 'tensor').astype(jnp.float32)  42.3 us
    all_to_all x1, waiting for transfers between devices, on_device(): lax.all_to_all(returned, 'expert', split_axis=0, concat_axis=0, tiled=True)  25.9 us
    all_to_all x1, starting transfers between devices, on_device(): lax.all_to_all(sent_d, 'expert', split_axis=0, concat_axis=0, tiled=True)  20.3 us
    all_to_all x1, starting transfers between devices, on_device(): lax.all_to_all(sent_x, 'expert', split_axis=0, concat_axis=0, tiled=True)  8.39 us
    scatter-add x1, other arithmetic, on_device(): jax.ops.segment_sum(masked, owner, num_segments=tok_count)  8.29 us
    all_to_all x1, starting transfers between devices, on_device(): lax.all_to_all(returned, 'expert', split_axis=0, concat_axis=0, tiled=True)  6.85 us
  transfers between devices with their start and end apart: 4, of which 4 were waited for; matrix products, arithmetic and copies ran while one was open for 12% of the time, Pallas kernels for 0%

commit v1 on v0

--- a/solution.py
+++ b/solution.py
@@ -1,9 +1,12 @@
 import jax
 import jax.numpy as jnp
 from jax import lax
+from jax.experimental import pallas as pl
+from jax.experimental.pallas import tpu as pltpu
 from jax.sharding import PartitionSpec as P
 
 TOP = 8
+MESH = pl.DeviceIdType.MESH
 
 
 def expert_backward(rows_x, rows_d, w_gate, w_up, w_down):
@@ -82,9 +85,419 @@
     return (grad_tokens, grad_gate, grad_up, grad_down)
 
 
+def merge_kernel(
+    tok_ref, cot_ref, gate_ref, wg_ref, wu_ref, wd_ref,
+    out_ref, gg_ref, gu_ref, gd_ref,
+    xs, ds_, wgu, wd, pre, hgrad, act, hid, act_t, hid_t, part, sib_out, sib_in, from_last, from_z, from_first,
+    stage, load_sem, send, recv, sib_send, sib_recv, last_send, last_recv, z_send, z_recv, first_send, first_recv, out_sem,
+):
+    rows = tok_ref.shape[0]
+    half = tok_ref.shape[1]
+    hidden = wg_ref.shape[1]
+    plane_rows = 4 * rows
+    f32 = jnp.float32
+    e, c = lax.axis_index("expert"), lax.axis_index("tensor")
+    x, y, z = e % 2, (e // 2) % 2, e // 4
+    a, b = x + c * (y - x), y + c * (x - y)
+
+    def index(aa, bb, zz):
+        return zz * 4 + aa * (1 + c) + bb * (2 - c)
+
+    def where(expert, core):
+        return dict(device_id={"expert": expert, "tensor": core}, device_id_type=MESH)
+
+    first, last = index(1 - a, b, z), index(a, 1 - b, z)
+    up, down = e + 4, e - 4
+    bufs = (xs, ds_)
+
+    loads = []
+    for t, ref in enumerate((tok_ref, cot_ref)):
+        loads.append(pltpu.make_async_copy(
+            ref, bufs[t].at[c, pl.ds(pl.multiple_of(e * rows, 16), rows), pl.ds(0, half)], load_sem.at[t]))
+    n = 2
+    weights = []
+    for h in range(2):
+        cols = pl.ds(h * half, half)
+        weights.append(pltpu.make_async_copy(wg_ref.at[0, :, cols], wgu.at[h, pl.ds(0, hidden)], load_sem.at[n]))
+        weights.append(pltpu.make_async_copy(wu_ref.at[0, :, cols], wgu.at[h, pl.ds(hidden, hidden)], load_sem.at[n + 1]))
+        weights.append(pltpu.make_async_copy(wd_ref.at[0, :, cols], wd.at[h], load_sem.at[n + 2]))
+        n += 3
+    for copy in loads + weights:
+        copy.start()
+    ds_[c, pl.ds(pl.multiple_of(e * rows, 16), rows), half:] = gate_ref[...]
+
+    barrier = pltpu.get_barrier_semaphore()
+    pl.semaphore_signal(barrier, inc=1, **where(first, c))
+    pl.semaphore_signal(barrier, inc=1, **where(last, c))
+    pl.semaphore_signal(barrier, inc=1, **where(e, 1 - c))
+
+    @pl.when(z < 3)
+    def _():
+        pl.semaphore_signal(barrier, inc=1, **where(up, c))
+
+    @pl.when(z > 0)
+    def _():
+        pl.semaphore_signal(barrier, inc=1, **where(down, c))
+
+    pl.semaphore_wait(barrier, 4 + (z + 1) // 2 % 2)
+    for copy in loads:
+        copy.wait()
+
+    def gather_copy(t, kind, blk, core):
+        target = (first, up, down, last, e)[kind]
+        view = bufs[t].at[core, pl.ds(pl.multiple_of(blk * rows, 16), rows)]
+        return pltpu.make_async_remote_copy(
+            src_ref=view, dst_ref=view, send_sem=send.at[t, kind, blk], recv_sem=recv.at[t, kind // 4, blk],
+            **where(target, 1 - c if kind == 4 else c))
+
+    def arrive(t, blk):
+        gather_copy(t, 0, blk, c).wait_recv()
+
+    def pass_on(t, blk, kinds):
+        for kind in kinds:
+            copy = gather_copy(t, kind, blk, c)
+            if kind == 1:
+                pl.when(z < 3)(copy.start)
+            elif kind == 2:
+                pl.when(z > 0)(copy.start)
+            else:
+                copy.start()
+
+    def own(t):
+        pass_on(t, e, (0, 1, 2, 3, 4))
+
+    def first_step(t):
+        blk = index(1 - a, b, z)
+        arrive(t, blk)
+        pass_on(t, blk, (1, 2, 3, 4))
+
+    def z_step(t, k):
+        for aa in (a, 1 - a):
+            @pl.when(z >= k)
+            def _():
+                blk = index(aa, b, z - k)
+                arrive(t, blk)
+                pass_on(t, blk, (1, 3, 4))
+
+            @pl.when(z + k <= 3)
+            def _():
+                blk = index(aa, b, z + k)
+                arrive(t, blk)
+                pass_on(t, blk, (2, 3, 4))
+
+    def last_step(t, k):
+        for aa in (a, 1 - a):
+            if k == 0:
+                arrive(t, index(aa, 1 - b, z))
+                pass_on(t, index(aa, 1 - b, z), (4,))
+                continue
+
+            @pl.when(z >= k)
+            def _():
+                arrive(t, index(aa, 1 - b, z - k))
+                pass_on(t, index(aa, 1 - b, z - k), (4,))
+
+            @pl.when(z + k <= 3)
+            def _():
+                arrive(t, index(aa, 1 - b, z + k))
+                pass_on(t, index(aa, 1 - b, z + k), (4,))
+
+    def sibling_step(t):
+        @pl.loop(0, 16)
+        def _(blk):
+            gather_copy(t, 4, blk, 1 - c).wait_recv()
+
+    def gather_sent(t):
+        def wait(blk, kinds):
+            for kind in kinds:
+                copy = gather_copy(t, kind, blk, c)
+                if kind == 1:
+                    pl.when(z < 3)(copy.wait_send)
+                elif kind == 2:
+                    pl.when(z > 0)(copy.wait_send)
+                else:
+                    copy.wait_send()
+
+        wait(e, (0, 1, 2, 3, 4))
+        wait(index(1 - a, b, z), (1, 2, 3, 4))
+        for k in range(1, 4):
+            for aa in (a, 1 - a):
+                pl.when(z >= k)(lambda: wait(index(aa, b, z - k), (1, 3, 4)))
+                pl.when(z + k <= 3)(lambda: wait(index(aa, b, z + k), (2, 3, 4)))
+
+        @pl.loop(0, 4)
+        def _(zz):
+            for aa in range(2):
+                gather_copy(t, 4, index(aa, 1 - b, zz), c).wait_send()
+
+    def plane_view(zz):
+        return pl.ds(pl.multiple_of(zz * plane_rows, 16), plane_rows)
+
+    contract_last = (((1,), (1,)), ((), ()))
+
+    def forward(zz):
+        at = plane_view(zz)
+
+        @pl.loop(0, 2 * hidden // 256)
+        def _(j):
+            cols = pl.ds(pl.multiple_of(j * 256, 256), 256)
+            pre[at, cols] = lax.dot_general(
+                xs[0, at, :], wgu[0, cols, :], contract_last, preferred_element_type=f32
+            ) + lax.dot_general(xs[1, at, :], wgu[1, cols, :], contract_last, preferred_element_type=f32)
+
+    own(0)
+    first_step(0)
+    z_step(0, 1)
+    own(1)
+    last_step(0, 0)
+    z_step(0, 2)
+    last_step(0, 1)
+    z_step(0, 3)
+    first_step(1)
+    last_step(0, 2)
+    z_step(1, 1)
+    last_step(0, 3)
+    for copy in weights:
+        copy.wait()
+    last_step(1, 0)
+    sibling_step(0)
+    forward(0)
+    z_step(1, 2)
+    forward(1)
+    last_step(1, 1)
+    z_step(1, 3)
+    forward(2)
+    last_step(1, 2)
+    forward(3)
+    last_step(1, 3)
+    sibling_step(1)
+
+    def plane_of(q):
+        swapped = (0, 1, 3, 2)[q]
+        turn = q + ((z + 1) // 2 % 2) * (swapped - q)
+        high = z // 2
+        return high * turn + (1 - high) * (3 - turn)
+
+    def sibling_copy(zz):
+        at = plane_view(zz)
+        return pltpu.make_async_remote_copy(
+            src_ref=sib_out.at[at], dst_ref=sib_in.at[at], send_sem=sib_send.at[zz], recv_sem=sib_recv.at[zz],
+            **where(e, 1 - c))
+
+    def backward(zz):
+        at = plane_view(zz)
+        hgrad[...] = lax.dot_general(
+            ds_[0, at, pl.ds(0, half)], wd[0], contract_last, preferred_element_type=f32
+        ) + lax.dot_general(ds_[1, at, pl.ds(0, half)], wd[1], contract_last, preferred_element_type=f32)
+
+        @pl.loop(0, 4)
+        def _(i):
+            here = pl.ds(pl.multiple_of(zz * plane_rows + i * rows, 16), rows)
+            lane = lax.broadcasted_iota(jnp.int32, (rows, 128), 1)
+            pieces = ds_[0, here, pl.ds(half, 128)].astype(f32)
+            weight = jnp.sum(jnp.where(jnp.bitwise_and(lane, 15) == e, pieces, 0.0), axis=1, keepdims=True)
+            gate_pre, up_pre = pre[here, pl.ds(0, hidden)], pre[here, pl.ds(hidden, hidden)]
+            sigmoid = 1.0 / (1.0 + jnp.exp(-gate_pre))
+            active = gate_pre * sigmoid
+            grad = hgrad[pl.ds(pl.multiple_of(i * rows, 16), rows), :] * weight
+            hid[here, :] = (active * up_pre * weight).astype(jnp.bfloat16)
+            act[here, pl.ds(hidden, hidden)] = (grad * active).astype(jnp.bfloat16)
+            act[here, pl.ds(0, hidden)] = (
+                grad * up_pre * sigmoid * (1.0 + gate_pre * (1.0 - sigmoid))).astype(jnp.bfloat16)
+
+        for side, dest in ((1 - c, sib_out), (c, part)):
+            @pl.loop(0, half // 512)
+            def _(j):
+                cols = pl.ds(pl.multiple_of(j * 512, 512), 512)
+                dest[at, cols] = jnp.dot(
+                    act[at, :], wgu[side, :, cols], preferred_element_type=f32).astype(jnp.bfloat16)
+            if dest is sib_out:
+                sibling_copy(zz).start()
+
+    def add_rows(dest, start, count, sources):
+        @pl.loop(0, count // 16)
+        def _(i):
+            here = pl.ds(pl.multiple_of(start + i * 16, 16), 16)
+            total = dest[here, :].astype(f32)
+            for ref, lead, offset in sources:
+                there = pl.ds(pl.multiple_of(offset + i * 16, 16), 16)
+                total = total + (ref[there, :] if lead is None else ref[lead, there, :]).astype(f32)
+            dest[here, :] = total.astype(jnp.bfloat16)
+
+    def block(blk):
+        return pl.ds(pl.multiple_of(blk * rows, 16), rows)
+
+    def last_copy(zz, aa):
+        slot = zz * 2 + aa
+        return pltpu.make_async_remote_copy(
+            src_ref=part.at[block(index(aa, 1 - b, zz))], dst_ref=from_last.at[slot],
+            send_sem=last_send.at[slot], recv_sem=last_recv.at[slot], **where(last, c))
+
+    def z_copy(way, zz, aa):
+        slot = way * 8 + zz * 2 + aa
+        return pltpu.make_async_remote_copy(
+            src_ref=part.at[block(index(aa, b, zz))], dst_ref=from_z.at[slot],
+            send_sem=z_send.at[slot], recv_sem=z_recv.at[slot], **where(down if way else up, c))
+
+    def reduce_last(zz):
+        sibling_copy(zz).wait_recv()
+        add_rows(part, zz * plane_rows, plane_rows, [(sib_in, None, zz * plane_rows)])
+        for aa in range(2):
+            last_copy(zz, aa).start()
+
+    def reduce_z(zz, final):
+        for aa in range(2):
+            start = index(aa, b, zz) * rows
+            last_copy(zz, aa).wait_recv()
+            add_rows(part, start, rows, [(from_last, zz * 2 + aa, 0)])
+            for way in range(2):
+                reached = (z > 0) if way == 0 else (z < 3)
+                ours = True if final else (zz > z if way == 0 else zz < z)
+
+                @pl.when(jnp.logical_and(reached, ours))
+                def _():
+                    z_copy(way, zz, aa).wait_recv()
+                    add_rows(part, start, rows, [(from_z, way * 8 + zz * 2 + aa, 0)])
+
+                if not final:
+                    pl.when(ours)(z_copy(way, zz, aa).start)
+
+    def first_copy():
+        return pltpu.make_async_remote_copy(
+            src_ref=part.at[block(first)], dst_ref=from_first, send_sem=first_send, recv_sem=first_recv,
+            **where(first, c))
+
+    outs = (gg_ref, gu_ref, gd_ref)
+
+    def weight_grad(m, h):
+        lhs = act_t if m < 2 else hid_t
+        base = m * hidden if m < 2 else 0
+        rhs = xs if m < 2 else ds_
+
+        @pl.loop(0, half // 512)
+        def _(j):
+            cols = pl.ds(pl.multiple_of(j * 512, 512), 512)
+            stage[m, h, :, cols] = jnp.dot(
+                lhs[pl.ds(base, hidden), :], rhs[h, :, cols], preferred_element_type=f32).astype(jnp.bfloat16)
+
+        weight_copy(m, h).start()
+
+    def weight_copy(m, h):
+        return pltpu.make_async_copy(
+            stage.at[m, h], outs[m].at[0, :, pl.ds(h * half, half)], out_sem.at[m, h])
+
+    planes = [plane_of(q) for q in range(4)]
+    backward(planes[0])
+    backward(planes[1])
+    reduce_last(planes[0])
+    backward(planes[2])
+    reduce_last(planes[1])
+    reduce_z(planes[0], False)
+    backward(planes[3])
+    reduce_last(planes[2])
+    reduce_z(planes[1], False)
+    reduce_last(planes[3])
+    act_t[...] = act[...].T
+    weight_grad(0, 0)
+    weight_grad(0, 1)
+    reduce_z(planes[2], False)
+    weight_grad(1, 0)
+    weight_grad(1, 1)
+    hid_t[...] = hid[...].T
+    weight_grad(2, 0)
+    weight_grad(2, 1)
+    reduce_z(planes[3], True)
+    first_copy().start()
+    first_copy().wait_recv()
+
+    @pl.loop(0, rows // 16)
+    def _(i):
+        here = pl.ds(pl.multiple_of(i * 16, 16), 16)
+        mine = pl.ds(pl.multiple_of(e * rows + i * 16, 16), 16)
+        out_ref[here, :] = (part[mine, :].astype(f32) + from_first[here, :].astype(f32)).astype(jnp.bfloat16)
+
+    for m in range(3):
+        for h in range(2):
+            weight_copy(m, h).wait()
+    first_copy().wait_send()
+    for q in range(4):
+        sibling_copy(planes[q]).wait_send()
+        for aa in range(2):
+            last_copy(planes[q], aa).wait_send()
+            if q < 3:
+                pl.when(planes[q] > z)(z_copy(0, planes[q], aa).wait_send)
+                pl.when(planes[q] < z)(z_copy(1, planes[q], aa).wait_send)
+    gather_sent(0)
+    gather_sent(1)
+
+
+def on_device_tree(tokens, cotangent, expert_ids, gate_values, w_gate, w_up, w_down):
+    rows, half = tokens.shape
+    hidden = w_gate.shape[1]
+    experts = lax.axis_size("expert")
+    total = rows * experts
+    chosen = expert_ids[:, :, None] == jnp.arange(experts, dtype=jnp.int32)[None, None, :]
+    dense = jnp.sum(jnp.where(chosen, gate_values[:, :, None], 0.0), axis=1)
+    high = lax.reduce_precision(dense, 8, 7)
+    middle = lax.reduce_precision(dense - high, 8, 7)
+    low = dense - high - middle
+    gates = jnp.concatenate(
+        [high, middle, low, jnp.zeros((rows, 128 - 3 * experts), jnp.float32)], axis=1).astype(jnp.bfloat16)
+    bf16, f32 = jnp.bfloat16, jnp.float32
+    any_, vmem = pl.BlockSpec(memory_space=pl.ANY), pl.BlockSpec(memory_space=pltpu.VMEM)
+    dma = pltpu.SemaphoreType.DMA
+    return tuple(pl.pallas_call(
+        merge_kernel,
+        out_shape=(
+            jax.ShapeDtypeStruct(tokens.shape, bf16),
+            jax.ShapeDtypeStruct(w_gate.shape, bf16),
+            jax.ShapeDtypeStruct(w_up.shape, bf16),
+            jax.ShapeDtypeStruct(w_down.shape, bf16),
+        ),
+        in_specs=[any_, any_, vmem, any_, any_, any_],
+        out_specs=(vmem, any_, any_, any_),
+        scratch_shapes=[
+            pltpu.VMEM((2, total, half), bf16),
+            pltpu.VMEM((2, total, half + 128), bf16),
+            pltpu.VMEM((2, 2 * hidden, half), bf16),
+            pltpu.VMEM((2, hidden, half), bf16),
+            pltpu.VMEM((total, 2 * hidden), f32),
+            pltpu.VMEM((4 * rows, hidden), f32),
+            pltpu.VMEM((total, 2 * hidden), bf16),
+            pltpu.VMEM((total, hidden), bf16),
+            pltpu.VMEM((2 * hidden, total), bf16),
+            pltpu.VMEM((hidden, total), bf16),
+            pltpu.VMEM((total, half), bf16),
+            pltpu.VMEM((total, half), bf16),
+            pltpu.VMEM((total, half), bf16),
+            pltpu.VMEM((8, rows, half), bf16),
+            pltpu.VMEM((16, rows, half), bf16),
+            pltpu.VMEM((rows, half), bf16),
+            pltpu.VMEM((3, 2, hidden, half), bf16),
+            dma((8,)),
+            dma((2, 5, 16)),
+            dma((2, 2, 16)),
+            dma((4,)),
+            dma((4,)),
+            dma((8,)),
+            dma((8,)),
+            dma((16,)),
+            dma((16,)),
+            dma,
+            dma,
+            dma((3, 2)),
+        ],
+        compiler_params=pltpu.CompilerParams(
+            collective_id=0, has_side_effects=True, vmem_limit_bytes=62 * 1024 * 1024),
+        cost_estimate=pl.CostEstimate(
+            flops=16 * total * hidden * 2 * half, bytes_accessed=24 * hidden * half, transcendentals=total * hidden),
+    )(tokens, cotangent, gates, w_gate, w_up, w_down))
+
+
 def solution(mesh):
+    tree = mesh.shape["expert"] == 16 and mesh.shape["tensor"] == 2
     return jax.shard_map(
-        on_device,
+        on_device_tree if tree else on_device,
         mesh=mesh,
         in_specs=(
             P("expert", "tensor"),

time: 339 us -> 135 us (0.40); the launches traced: 334 us -> 135 us
  waiting for transfers between devices: 203 us -> 0 us
  Pallas kernels: 0 us -> 122 us
  matrix products: 41 us -> 0 us
  starting transfers between devices: 35.7 us -> 0 us
  other arithmetic: 24.6 us -> 1.42 us
  between operations: 14.2 us -> 0.66 us
  blocking collectives: 4.71 us -> 0 us
    all_to_all x3 -> x0, waiting for transfers between devices: 161 us -> none  [the longest x1 67.7 us: on_device(): lax.all_to_all(sent_x, 'expert', split_axis=0, concat_axis=0, tiled=True)]
    pallas_call x0 -> x1, Pallas kernels: none -> 122 us  [on_device_tree(): pl.pallas_call(merge_kernel, out_shape=(jax.ShapeDtypeStruct(tokens.shape...]
    psum x1 -> x0, waiting for transfers between devices: 42.3 us -> none  [on_device(): lax.psum(partial_value.astype(jnp.bfloat16), 'tensor').astype(jnp.float32)]
    dot_general x8 -> x0, matrix products: 41 us -> none  [the longest x1 5.99 us: expert_backward(): jnp.einsum('secd,ehd->sech', rows_d, w_down, preferred_element_type=jnp.f...]
    all_to_all x3 -> x0, starting transfers between devices: 35.5 us -> none  [the longest x1 20.3 us: on_device(): lax.all_to_all(sent_d, 'expert', split_axis=0, concat_axis=0, tiled=True)]
    convert_element_type x4 -> x0, other arithmetic: 9.52 us -> none  [the longest x1 5.61 us: on_device(): (slot_weight[:, None] * full_d[owner].astype(jnp.float32)).astype(jnp.bfl...]
    unnamed x24 -> x8, local copies, waits for them, and re-layouts: 1.25 us -> 10.4 us
    gather x2 -> x0, local copies, waits for them, and re-layouts: 8.73 us -> none  [the longest x1 4.38 us: on_device(): full_d[owner].astype(jnp.float32)]
  transfers between devices with their start and end apart: 4 -> 0, of which waited for: 4 -> 0; matrix products, arithmetic and copies ran while one was open for 12% -> 0% of each run, Pallas kernels for 0% -> 0%
where the time goes in v1:
time: 135 us
  Pallas kernels  122 us (90%)
  local copies, waits for them, and re-layouts  10.6 us (8%)
  other arithmetic  1.42 us (1%)
    pallas_call x1, Pallas kernels, on_device_tree(): pl.pallas_call(merge_kernel, out_shape=(jax.ShapeDtypeStruct(tokens.shape...  122 us
    unnamed x8, local copies, waits for them, and re-layouts  10.4 us

profile of v1, /device:TPU:0, one launch (start us, length us, event | category | flops | bytes accessed | tf_op | source)
XLA Modules:
  0.0 134.6 jit_solution(6628441208242812486)
XLA Ops:
  0.6 0.1 pad.3.clone
  0.7 0.7 select_reduce_fusion
  1.5 0.1 copy.16
  1.5 0.1 copy.15
  1.6 0.7 maximum_maximum_fusion.gate_ref
  2.3 121.9 %shard_map.102 = (bf16[48,2048]{1,0:T(8,128)(2,1)}, bf16[1,384,4096]{2,1,0:T(8,128)(2,1)}, bf16[1,384,4096]{2,1,0:T(8,128)(2,1)}, bf16[1,384,4096]{2,1,0:T(8,128)(2,1)}) custom-call(bf16[48,2048]{1,0:T(8,128)(2,1)} %tok_ref.1, bf16[48,2048]{1,0:T(8,128)(2,1)} %cot_ref.1, bf16[48,128]{1,0:T(8,128)(2,1)} %maximum_maximum_fusion.gate_ref, ...), custom_call_target="tpu_custom_call" | custom-call | flops 19327352832 | bytes 18874368 | tf_op jit(solution)/shard_map/pallas_call | solution.py:449
  124.2 1.6 %copy.22 = bf16[48,2048]{1,0:T(8,128)(2,1)} copy(bf16[48,2048]{1,0:T(8,128)(2,1)} %get-tuple-element.11) | data formatting | bytes 393216
  125.8 0.0 copy-start.1
  125.8 4.1 %copy.23 = bf16[1,384,4096]{2,1,0:T(8,128)(2,1)} copy(bf16[1,384,4096]{2,1,0:T(8,128)(2,1)} %get-tuple-element.12) | data formatting | bytes 6291456
  129.9 0.0 copy-done.1
  129.9 0.0 copy-start
  129.9 1.7 %copy.24 = bf16[1,384,4096]{2,1,0:T(8,128)(2,1)} copy(bf16[1,384,4096]{2,1,0:T(8,128)(2,1)S(1)} %copy-done.1) | data formatting | bytes 6291456
  131.6 1.4 %copy-done = bf16[1,384,4096]{2,1,0:T(8,128)(2,1)S(1)} copy-done((bf16[1,384,4096]{2,1,0:T(8,128)(2,1)S(1)}, bf16[1,384,4096]{2,1,0:T(8,128)(2,1)}, u32[]{:S(2)}) %copy-start) | copy-done | bytes 3145752
  132.9 1.7 %copy.25 = bf16[1,384,4096]{2,1,0:T(8,128)(2,1)} copy(bf16[1,384,4096]{2,1,0:T(8,128)(2,1)S(1)} %copy-done) | data formatting | bytes 6291456
  (3 shorter events, 0.0 us)
Async XLA Ops:
  125.8 4.1 %copy-start.1 = (bf16[1,384,4096]{2,1,0:T(8,128)(2,1)S(1)}, bf16[1,384,4096]{2,1,0:T(8,128)(2,1)}, u32[]{:S(2)}) copy-start(bf16[1,384,4096]{2,1,0:T(8,128)(2,1)} %get-tuple-element.13) | copy-start | bytes 9437188
  129.9 3.0 %copy-start = (bf16[1,384,4096]{2,1,0:T(8,128)(2,1)S(1)}, bf16[1,384,4096]{2,1,0:T(8,128)(2,1)}, u32[]{:S(2)}) copy-start(bf16[1,384,4096]{2,1,0:T(8,128)(2,1)} %get-tuple-element.14) | copy-start | bytes 9437188

commit v2 on v0

--- a/solution.py
+++ b/solution.py
@@ -1,9 +1,14 @@
+import functools
+
 import jax
 import jax.numpy as jnp
 from jax import lax
+from jax.experimental import pallas as pl
+from jax.experimental.pallas import tpu as pltpu
 from jax.sharding import PartitionSpec as P
 
 TOP = 8
+MESH = pl.DeviceIdType.MESH
 
 
 def expert_backward(rows_x, rows_d, w_gate, w_up, w_down):
@@ -82,9 +87,473 @@
     return (grad_tokens, grad_gate, grad_up, grad_down)
 
 
+def merge_kernel(
+    sizes, tok_ref, cot_ref, gate_ref, wg_ref, wu_ref, wd_ref,
+    out_ref, gg_ref, gu_ref, gd_ref,
+    xs, ds_, wgu, wd, pre, hgrad, act, hid, act_t, hid_t, part, sib_out, sib_in, from_last, from_z, from_first,
+    load_sem, send, recv, sib_send, sib_recv, last_send, last_recv, z_send, z_recv, first_send, first_recv, out_sem,
+):
+    half = tok_ref.shape[1]
+    hidden = wg_ref.shape[1]
+    f32 = jnp.float32
+    starts = (0, sizes[0])
+    e, c = lax.axis_index("expert"), lax.axis_index("tensor")
+    x, y, z = e % 2, (e // 2) % 2, e // 4
+    a, b = x + c * (y - x), y + c * (x - y)
+
+    def index(aa, bb, zz):
+        return zz * 4 + aa * (1 + c) + bb * (2 - c)
+
+    def where(expert, core):
+        return dict(device_id={"expert": expert, "tensor": core}, device_id_type=MESH)
+
+    first, last = index(1 - a, b, z), index(a, 1 - b, z)
+    up, down = e + 4, e - 4
+    bufs = (xs, ds_)
+
+    def block(j, blk):
+        return pl.ds(pl.multiple_of(blk * sizes[j], 16), sizes[j])
+
+    loads = []
+    for t, ref in enumerate((tok_ref, cot_ref)):
+        for j in range(2):
+            loads.append(pltpu.make_async_copy(
+                ref.at[pl.ds(starts[j], sizes[j])],
+                bufs[t][j].at[c, block(j, e), pl.ds(0, half)], load_sem.at[t * 2 + j]))
+    n = 4
+    weights = []
+    for h in range(2):
+        cols = pl.ds(h * half, half)
+        weights.append(pltpu.make_async_copy(wg_ref.at[0, :, cols], wgu.at[h, pl.ds(0, hidden)], load_sem.at[n]))
+        weights.append(pltpu.make_async_copy(wu_ref.at[0, :, cols], wgu.at[h, pl.ds(hidden, hidden)], load_sem.at[n + 1]))
+        weights.append(pltpu.make_async_copy(wd_ref.at[0, :, cols], wd.at[h], load_sem.at[n + 2]))
+        n += 3
+    for copy in loads + weights:
+        copy.start()
+    for j in range(2):
+        ds_[j][c, block(j, e), half:] = gate_ref[starts[j]:starts[j] + sizes[j], :]
+
+    barrier = pltpu.get_barrier_semaphore()
+    pl.semaphore_signal(barrier, inc=1, **where(first, c))
+    pl.semaphore_signal(barrier, inc=1, **where(last, c))
+    pl.semaphore_signal(barrier, inc=1, **where(e, 1 - c))
+
+    @pl.when(z < 3)
+    def _():
+        pl.semaphore_signal(barrier, inc=1, **where(up, c))
+
+    @pl.when(z > 0)
+    def _():
+        pl.semaphore_signal(barrier, inc=1, **where(down, c))
+
+    pl.semaphore_wait(barrier, 4 + (z + 1) // 2 % 2)
+    for copy in loads:
+        copy.wait()
+
+    def gather_copy(t, j, kind, blk, core):
+        target = (first, up, down, last, e)[kind]
+        view = bufs[t][j].at[core, block(j, blk)]
+        return pltpu.make_async_remote_copy(
+            src_ref=view, dst_ref=view, send_sem=send.at[t * 2 + j, kind, blk],
+            recv_sem=recv.at[t * 2 + j, kind // 4, blk], **where(target, 1 - c if kind == 4 else c))
+
+    def arrive(t, j, blk):
+        gather_copy(t, j, 0, blk, c).wait_recv()
+
+    def each(t, j, blk, kinds, verb):
+        for kind in kinds:
+            do = getattr(gather_copy(t, j, kind, blk, c), verb)
+            if kind == 1:
+                pl.when(z < 3)(do)
+            elif kind == 2:
+                pl.when(z > 0)(do)
+            else:
+                do()
+
+    def own(t, j):
+        each(t, j, e, (0, 1, 2, 3, 4), "start")
+
+    def first_step(t, j):
+        blk = index(1 - a, b, z)
+        arrive(t, j, blk)
+        each(t, j, blk, (1, 2, 3, 4), "start")
+
+    def z_step(t, j, k):
+        for aa in (a, 1 - a):
+            @pl.when(z >= k)
+            def _():
+                blk = index(aa, b, z - k)
+                arrive(t, j, blk)
+                each(t, j, blk, (1, 3, 4), "start")
+
+            @pl.when(z + k <= 3)
+            def _():
+                blk = index(aa, b, z + k)
+                arrive(t, j, blk)
+                each(t, j, blk, (2, 3, 4), "start")
+
+    def last_step(t, j, k):
+        def over(blk):
+            arrive(t, j, blk)
+            each(t, j, blk, (4,), "start")
+
+        for aa in (a, 1 - a):
+            if k == 0:
+                over(index(aa, 1 - b, z))
+                continue
+
+            @pl.when(z >= k)
+            def _():
+                over(index(aa, 1 - b, z - k))
+
+            @pl.when(z + k <= 3)
+            def _():
+                over(index(aa, 1 - b, z + k))
+
+    def sibling_step(t, j):
+        @pl.loop(0, 16)
+        def _(blk):
+            gather_copy(t, j, 4, blk, 1 - c).wait_recv()
+
+    def gather_sent(t, j):
+        each(t, j, e, (0, 1, 2, 3, 4), "wait_send")
+        each(t, j, index(1 - a, b, z), (1, 2, 3, 4), "wait_send")
+        for k in range(1, 4):
+            for aa in (a, 1 - a):
+                pl.when(z >= k)(lambda: each(t, j, index(aa, b, z - k), (1, 3, 4), "wait_send"))
+                pl.when(z + k <= 3)(lambda: each(t, j, index(aa, b, z + k), (2, 3, 4), "wait_send"))
+
+        @pl.loop(0, 4)
+        def _(zz):
+            for aa in range(2):
+                gather_copy(t, j, 4, index(aa, 1 - b, zz), c).wait_send()
+
+    contract_last = (((1,), (1,)), ((), ()))
+
+    def rows_of(j):
+        return pl.ds(starts[j] * 16, sizes[j] * 16)
+
+    def forward(j, lo, hi):
+        @pl.loop(lo, hi)
+        def _(i):
+            cols = pl.ds(pl.multiple_of(i * 256, 256), 256)
+            pre[rows_of(j), cols] = lax.dot_general(
+                xs[j][0], wgu[0, cols, :], contract_last, preferred_element_type=f32
+            ) + lax.dot_general(xs[j][1], wgu[1, cols, :], contract_last, preferred_element_type=f32)
+
+    def hidden_backward(j):
+        @pl.loop(0, sizes[j] * 16 // 256)
+        def _(i):
+            at = pl.ds(pl.multiple_of(i * 256, 256), 256)
+            hgrad[at, :] = lax.dot_general(
+                ds_[j][0, at, pl.ds(0, half)], wd[0], contract_last, preferred_element_type=f32
+            ) + lax.dot_general(ds_[j][1, at, pl.ds(0, half)], wd[1], contract_last, preferred_element_type=f32)
+
+        @pl.loop(0, sizes[j] * 16 // 64)
+        def _(i):
+            there = pl.ds(pl.multiple_of(i * 64, 64), 64)
+            here = pl.ds(pl.multiple_of(starts[j] * 16 + i * 64, 64), 64)
+            lane = lax.broadcasted_iota(jnp.int32, (64, 128), 1)
+            pieces = ds_[j][0, there, pl.ds(half, 128)].astype(f32)
+            weight = jnp.sum(jnp.where(jnp.bitwise_and(lane, 15) == e, pieces, 0.0), axis=1, keepdims=True)
+            gate_pre, up_pre = pre[here, pl.ds(0, hidden)], pre[here, pl.ds(hidden, hidden)]
+            sigmoid = 1.0 / (1.0 + jnp.exp(-gate_pre))
+            active = gate_pre * sigmoid
+            grad = hgrad[there, :] * weight
+            hid[here, :] = (active * up_pre * weight).astype(jnp.bfloat16)
+            act[here, pl.ds(hidden, hidden)] = (grad * active).astype(jnp.bfloat16)
+            act[here, pl.ds(0, hidden)] = (
+                grad * up_pre * sigmoid * (1.0 + gate_pre * (1.0 - sigmoid))).astype(jnp.bfloat16)
+
+    def row_backward(j, side, dest):
+        @pl.loop(0, half // 512)
+        def _(i):
+            cols = pl.ds(pl.multiple_of(i * 512, 512), 512)
+            dest[j][:, cols] = jnp.dot(
+                act[rows_of(j), :], wgu[side, :, cols], preferred_element_type=f32).astype(jnp.bfloat16)
+
+    def plane_of(q):
+        swapped = (0, 1, 3, 2)[q]
+        turn = q + ((z + 1) // 2 % 2) * (swapped - q)
+        high = z // 2
+        return high * turn + (1 - high) * (3 - turn)
+
+    planes = [plane_of(q) for q in range(4)]
+
+    def sibling_copy(j, zz):
+        at = pl.ds(pl.multiple_of(zz * 4 * sizes[j], 16), 4 * sizes[j])
+        return pltpu.make_async_remote_copy(
+            src_ref=sib_out[j].at[at], dst_ref=sib_in[j].at[at], send_sem=sib_send.at[j, zz],
+            recv_sem=sib_recv.at[j, zz], **where(e, 1 - c))
+
+    def row_backward_out(j):
+        row_backward(j, 1 - c, sib_out)
+        for zz in planes:
+            sibling_copy(j, zz).start()
+
+    def row_backward_own(j):
+        row_backward(j, c, part)
+
+    def add_rows(j, start, count, sources):
+        dest = part[j]
+
+        @pl.loop(0, count // 16)
+        def _(i):
+            here = pl.ds(pl.multiple_of(start + i * 16, 16), 16)
+            total = dest[here, :].astype(f32)
+            for ref, lead, offset in sources:
+                there = pl.ds(pl.multiple_of(offset + i * 16, 16), 16)
+                total = total + (ref[there, :] if lead is None else ref[lead, there, :]).astype(f32)
+            dest[here, :] = total.astype(jnp.bfloat16)
+
+    def last_copy(j, zz, aa):
+        slot = zz * 2 + aa
+        return pltpu.make_async_remote_copy(
+            src_ref=part[j].at[block(j, index(aa, 1 - b, zz))], dst_ref=from_last[j].at[slot],
+            send_sem=last_send.at[j, slot], recv_sem=last_recv.at[j, slot], **where(last, c))
+
+    def z_copy(j, way, zz, aa):
+        slot = way * 8 + zz * 2 + aa
+        return pltpu.make_async_remote_copy(
+            src_ref=part[j].at[block(j, index(aa, b, zz))], dst_ref=from_z[j].at[slot],
+            send_sem=z_send.at[j, slot], recv_sem=z_recv.at[j, slot], **where(down if way else up, c))
+
+    def reduce_last(j, q):
+        zz = planes[q]
+        sibling_copy(j, zz).wait_recv()
+        add_rows(j, zz * 4 * sizes[j], 4 * sizes[j], [(sib_in[j], None, zz * 4 * sizes[j])])
+        for aa in range(2):
+            last_copy(j, zz, aa).start()
+
+    def reduce_z(j, q):
+        zz, final = planes[q], q == 3
+        for aa in range(2):
+            start = index(aa, b, zz) * sizes[j]
+            last_copy(j, zz, aa).wait_recv()
+            add_rows(j, start, sizes[j], [(from_last[j], zz * 2 + aa, 0)])
+            for way in range(2):
+                reached = (z > 0) if way == 0 else (z < 3)
+                ours = True if final else (zz > z if way == 0 else zz < z)
+
+                @pl.when(jnp.logical_and(reached, ours))
+                def _():
+                    z_copy(j, way, zz, aa).wait_recv()
+                    add_rows(j, start, sizes[j], [(from_z[j], way * 8 + zz * 2 + aa, 0)])
+
+                if not final:
+                    pl.when(ours)(z_copy(j, way, zz, aa).start)
+
+    def first_copy(j):
+        return pltpu.make_async_remote_copy(
+            src_ref=part[j].at[block(j, first)], dst_ref=from_first[j], send_sem=first_send.at[j],
+            recv_sem=first_recv.at[j], **where(first, c))
+
+    def finish(j):
+        first_copy(j).wait_recv()
+
+        @pl.loop(0, sizes[j] // 16)
+        def _(i):
+            here = pl.ds(pl.multiple_of(i * 16, 16), 16)
+            mine = pl.ds(pl.multiple_of(e * sizes[j] + i * 16, 16), 16)
+            out_ref[pl.ds(pl.multiple_of(starts[j] + i * 16, 16), 16), :] = (
+                part[j][mine, :].astype(f32) + from_first[j][here, :].astype(f32)).astype(jnp.bfloat16)
+
+    outs = (gg_ref, gu_ref, gd_ref)
+
+    def weight_copy(m, h):
+        held = wgu.at[h, pl.ds(m * hidden, hidden)] if m < 2 else wd.at[h]
+        return pltpu.make_async_copy(held, outs[m].at[0, :, pl.ds(h * half, half)], out_sem.at[m, h])
+
+    def weight_grad(m, h):
+        lhs, rhs = (act_t, xs) if m < 2 else (hid_t, ds_)
+        base = m * hidden if m < 2 else 0
+
+        @pl.loop(0, half // 512)
+        def _(i):
+            cols = pl.ds(pl.multiple_of(i * 512, 512), 512)
+            total = jnp.dot(
+                lhs[pl.ds(base, hidden), rows_of(0)], rhs[0][h, :, cols], preferred_element_type=f32
+            ) + jnp.dot(lhs[pl.ds(base, hidden), rows_of(1)], rhs[1][h, :, cols], preferred_element_type=f32)
+            if m < 2:
+                wgu[h, pl.ds(base, hidden), cols] = total.astype(jnp.bfloat16)
+            else:
+                wd[h, :, cols] = total.astype(jnp.bfloat16)
+
+        weight_copy(m, h).start()
+
+    X, G = 0, 1
+    own(X, 0)
+    first_step(X, 0)
+    z_step(X, 0, 1)
+    own(G, 0)
+    last_step(X, 0, 0)
+    z_step(X, 0, 2)
+    last_step(X, 0, 1)
+    z_step(X, 0, 3)
+    first_step(G, 0)
+    last_step(X, 0, 2)
+    z_step(G, 0, 1)
+    last_step(X, 0, 3)
+    last_step(G, 0, 0)
+    own(X, 1)
+    for copy in weights:
+        copy.wait()
+    sibling_step(X, 0)
+    z_step(G, 0, 2)
+    forward(0, 0, 1)
+    last_step(G, 0, 1)
+    z_step(G, 0, 3)
+    first_step(X, 1)
+    own(G, 1)
+    forward(0, 1, 2)
+    last_step(G, 0, 2)
+    z_step(X, 1, 1)
+    forward(0, 2, 3)
+    last_step(G, 0, 3)
+    last_step(X, 1, 0)
+    sibling_step(G, 0)
+
+    hidden_backward(0)
+    z_step(X, 1, 2)
+    last_step(X, 1, 1)
+    first_step(G, 1)
+    row_backward_out(0)
+    z_step(X, 1, 3)
+    last_step(X, 1, 2)
+    z_step(G, 1, 1)
+    row_backward_own(0)
+    last_step(X, 1, 3)
+    last_step(G, 1, 0)
+    reduce_last(0, 0)
+    z_step(G, 1, 2)
+    reduce_last(0, 1)
+    last_step(G, 1, 1)
+    reduce_z(0, 0)
+    sibling_step(X, 1)
+    z_step(G, 1, 3)
+    reduce_last(0, 2)
+    reduce_z(0, 1)
+    last_step(G, 1, 2)
+    reduce_last(0, 3)
+    forward(1, 0, 3)
+    last_step(G, 1, 3)
+    reduce_z(0, 2)
+    sibling_step(G, 1)
+
+    hidden_backward(1)
+    row_backward_out(1)
+    row_backward_own(1)
+    reduce_last(1, 0)
+    reduce_last(1, 1)
+    reduce_z(0, 3)
+    first_copy(0).start()
+    reduce_last(1, 2)
+    reduce_z(1, 0)
+    reduce_last(1, 3)
+    act_t[...] = act[...].T
+    weight_grad(0, 0)
+    reduce_z(1, 1)
+    weight_grad(0, 1)
+    weight_grad(1, 0)
+    reduce_z(1, 2)
+    weight_grad(1, 1)
+    finish(0)
+    hid_t[...] = hid[...].T
+    reduce_z(1, 3)
+    first_copy(1).start()
+    weight_grad(2, 0)
+    weight_grad(2, 1)
+    finish(1)
+
+    for m in range(3):
+        for h in range(2):
+            weight_copy(m, h).wait()
+    for j in range(2):
+        first_copy(j).wait_send()
+        for q in range(4):
+            zz = planes[q]
+            sibling_copy(j, zz).wait_send()
+            for aa in range(2):
+                last_copy(j, zz, aa).wait_send()
+                if q < 3:
+                    pl.when(zz > z)(z_copy(j, 0, zz, aa).wait_send)
+                    pl.when(zz < z)(z_copy(j, 1, zz, aa).wait_send)
+        gather_sent(0, j)
+        gather_sent(1, j)
+
+
+def on_device_tree(tokens, cotangent, expert_ids, gate_values, w_gate, w_up, w_down):
+    rows, half = tokens.shape
+    hidden = w_gate.shape[1]
+    experts = lax.axis_size("expert")
+    total = rows * experts
+    sizes = (rows // 48 * 32, rows // 48 * 16)
+    chosen = expert_ids[:, :, None] == jnp.arange(experts, dtype=jnp.int32)[None, None, :]
+    dense = jnp.sum(jnp.where(chosen, gate_values[:, :, None], 0.0), axis=1)
+    high = lax.reduce_precision(dense, 8, 7)
+    middle = lax.reduce_precision(dense - high, 8, 7)
+    low = dense - high - middle
+    gates = jnp.concatenate(
+        [high, middle, low, jnp.zeros((rows, 128 - 3 * experts), jnp.float32)], axis=1).astype(jnp.bfloat16)
+    bf16, f32 = jnp.bfloat16, jnp.float32
+    any_, vmem = pl.BlockSpec(memory_space=pl.ANY), pl.BlockSpec(memory_space=pltpu.VMEM)
+    dma = pltpu.SemaphoreType.DMA
+    whole = tuple(size * experts for size in sizes)
+
+    def chunks(*shape):
+        return [pltpu.VMEM(tuple(n[j] if isinstance(n, tuple) else n for n in shape), bf16) for j in range(2)]
+
+    return tuple(pl.pallas_call(
+        functools.partial(merge_kernel, sizes),
+        out_shape=(
+            jax.ShapeDtypeStruct(tokens.shape, bf16),
+            jax.ShapeDtypeStruct(w_gate.shape, bf16),
+            jax.ShapeDtypeStruct(w_up.shape, bf16),
+            jax.ShapeDtypeStruct(w_down.shape, bf16),
+        ),
+        in_specs=[any_, any_, vmem, any_, any_, any_],
+        out_specs=(vmem, any_, any_, any_),
+        scratch_shapes=[
+            chunks(2, whole, half),
+            chunks(2, whole, half + 128),
+            pltpu.VMEM((2, 2 * hidden, half), bf16),
+            pltpu.VMEM((2, hidden, half), bf16),
+            pltpu.VMEM((total, 2 * hidden), f32),
+            pltpu.VMEM((whole[0], hidden), f32),
+            pltpu.VMEM((total, 2 * hidden), bf16),
+            pltpu.VMEM((total, hidden), bf16),
+            pltpu.VMEM((2 * hidden, total), bf16),
+            pltpu.VMEM((hidden, total), bf16),
+            chunks(whole, half),
+            chunks(whole, half),
+            chunks(whole, half),
+            chunks(8, sizes, half),
+            chunks(16, sizes, half),
+            chunks(sizes, half),
+            dma((10,)),
+            dma((4, 5, 16)),
+            dma((4, 2, 16)),
+            dma((2, 4)),
+            dma((2, 4)),
+            dma((2, 8)),
+            dma((2, 8)),
+            dma((2, 16)),
+            dma((2, 16)),
+            dma((2,)),
+            dma((2,)),
+            dma((3, 2)),
+        ],
+        compiler_params=pltpu.CompilerParams(
+            collective_id=0, has_side_effects=True, vmem_limit_bytes=43 * 1024 * 1024),
+        cost_estimate=pl.CostEstimate(
+            flops=16 * total * hidden * 2 * half, bytes_accessed=24 * hidden * half, transcendentals=total * hidden),
+    )(tokens, cotangent, gates, w_gate, w_up, w_down))
+
+
 def solution(mesh):
+    tree = mesh.shape["expert"] == 16 and mesh.shape["tensor"] == 2
     return jax.shard_map(
-        on_device,
+        on_device_tree if tree else on_device,
         mesh=mesh,
         in_specs=(
             P("expert", "tensor"),

time: 339 us -> 122 us (0.36); the launches traced: 334 us -> 121 us
  waiting for transfers between devices: 203 us -> 0 us
  Pallas kernels: 0 us -> 112 us
  matrix products: 41 us -> 0 us
  starting transfers between devices: 35.7 us -> 0 us
  other arithmetic: 24.6 us -> 0.82 us
  between operations: 14.2 us -> 0.67 us
  blocking collectives: 4.71 us -> 0 us
    all_to_all x3 -> x0, waiting for transfers between devices: 161 us -> none  [the longest x1 67.7 us: on_device(): lax.all_to_all(sent_x, 'expert', split_axis=0, concat_axis=0, tiled=True)]
    pallas_call x0 -> x1, Pallas kernels: none -> 112 us  [on_device_tree(): pl.pallas_call(functools.partial(merge_kernel, sizes), out_shape=(jax.Sha...]
    psum x1 -> x0, waiting for transfers between devices: 42.3 us -> none  [on_device(): lax.psum(partial_value.astype(jnp.bfloat16), 'tensor').astype(jnp.float32)]
    dot_general x8 -> x0, matrix products: 41 us -> none  [the longest x1 5.99 us: expert_backward(): jnp.einsum('secd,ehd->sech', rows_d, w_down, preferred_element_type=jnp.f...]
    all_to_all x3 -> x0, starting transfers between devices: 35.5 us -> none  [the longest x1 20.3 us: on_device(): lax.all_to_all(sent_d, 'expert', split_axis=0, concat_axis=0, tiled=True)]
    convert_element_type x4 -> x0, other arithmetic: 9.52 us -> none  [the longest x1 5.61 us: on_device(): (slot_weight[:, None] * full_d[owner].astype(jnp.float32)).astype(jnp.bfl...]
    gather x2 -> x0, local copies, waits for them, and re-layouts: 8.73 us -> none  [the longest x1 4.38 us: on_device(): full_d[owner].astype(jnp.float32)]
    scatter-add x1 -> x0, other arithmetic: 8.29 us -> none  [on_device(): jax.ops.segment_sum(masked, owner, num_segments=tok_count)]
  transfers between devices with their start and end apart: 4 -> 0, of which waited for: 4 -> 0; matrix products, arithmetic and copies ran while one was open for 12% -> 0% of each run, Pallas kernels for 0% -> 0%
where the time goes in v2:
time: 122 us; the launch traced here: 121 us
  Pallas kernels  112 us (92%)
  local copies, waits for them, and re-layouts  7.76 us (6%)
    pallas_call x1, Pallas kernels, on_device_tree(): pl.pallas_call(functools.partial(merge_kernel, sizes), out_shape=(jax.Sha...  112 us
    unnamed x8, local copies, waits for them, and re-layouts  7.52 us

profile of v2, /device:TPU:0, one launch (start us, length us, event | category | flops | bytes accessed | tf_op | source)
XLA Modules:
  0.0 121.4 jit_solution(9292688722416049407)
XLA Ops:
  0.6 0.1 pad.3.clone
  0.7 0.7 select_reduce_fusion
  1.5 0.1 copy.16
  1.5 0.1 copy.15
  1.6 0.1 maximum_maximum_fusion.gate_ref
  1.7 0.0 copy-start
  1.7 0.9 copy-done
  2.6 0.0 copy-start.1
  2.6 0.9 copy-done.1
  3.6 112.2 %shard_map.102 = (bf16[48,2048]{1,0:T(8,128)(2,1)S(1)}, bf16[1,384,4096]{2,1,0:T(8,128)(2,1)S(1)}, bf16[1,384,4096]{2,1,0:T(8,128)(2,1)S(1)}, bf16[1,384,4096]{2,1,0:T(8,128)(2,1)S(1)}) custom-call(bf16[48,2048]{1,0:T(8,128)(2,1)S(1)} %copy-done, bf16[48,2048]{1,0:T(8,128)(2,1)S(1)} %copy-done.1, bf16[48,128]{1,0:T(8,128)(2,1)S(1)} %maximum_maximum_fusion.gate_ref, ...), custom_call_target="tpu_custom_call" | custom-call | flops 19327352832 | bytes 18874368 | tf_op jit(solution)/shard_map/pallas_call | solution.py:506
  115.8 0.7 copy.22
  116.4 1.7 %copy.23 = bf16[1,384,4096]{2,1,0:T(8,128)(2,1)} copy(bf16[1,384,4096]{2,1,0:T(8,128)(2,1)S(1)} %get-tuple-element.12) | data formatting | bytes 6291456
  118.1 1.7 %copy.24 = bf16[1,384,4096]{2,1,0:T(8,128)(2,1)} copy(bf16[1,384,4096]{2,1,0:T(8,128)(2,1)S(1)} %get-tuple-element.13) | data formatting | bytes 6291456
  119.8 1.7 %copy.25 = bf16[1,384,4096]{2,1,0:T(8,128)(2,1)} copy(bf16[1,384,4096]{2,1,0:T(8,128)(2,1)S(1)} %get-tuple-element.14) | data formatting | bytes 6291456
  (3 shorter events, 0.0 us)
Async XLA Ops:
  1.7 0.9 copy-start
  2.6 0.9 copy-start.1

commit v3 on v2

--- a/solution.py
+++ b/solution.py
@@ -91,12 +91,13 @@
     sizes, tok_ref, cot_ref, gate_ref, wg_ref, wu_ref, wd_ref,
     out_ref, gg_ref, gu_ref, gd_ref,
     xs, ds_, wgu, wd, pre, hgrad, act, hid, act_t, hid_t, part, sib_out, sib_in, from_last, from_z, from_first,
-    load_sem, send, recv, sib_send, sib_recv, last_send, last_recv, z_send, z_recv, first_send, first_recv, out_sem,
+    acc, load_sem, send, recv, sib_send, sib_recv, last_send, last_recv, z_send, z_recv, first_send, first_recv, out_sem,
 ):
     half = tok_ref.shape[1]
     hidden = wg_ref.shape[1]
     f32 = jnp.float32
-    starts = (0, sizes[0])
+    count = len(sizes)
+    starts = tuple(sum(sizes[:j]) for j in range(count))
     e, c = lax.axis_index("expert"), lax.axis_index("tensor")
     x, y, z = e % 2, (e // 2) % 2, e // 4
     a, b = x + c * (y - x), y + c * (x - y)
@@ -116,11 +117,11 @@
 
     loads = []
     for t, ref in enumerate((tok_ref, cot_ref)):
-        for j in range(2):
+        for j in range(count):
             loads.append(pltpu.make_async_copy(
                 ref.at[pl.ds(starts[j], sizes[j])],
-                bufs[t][j].at[c, block(j, e), pl.ds(0, half)], load_sem.at[t * 2 + j]))
-    n = 4
+                bufs[t][j].at[c, block(j, e), pl.ds(0, half)], load_sem.at[t * count + j]))
+    n = 2 * count
     weights = []
     for h in range(2):
         cols = pl.ds(h * half, half)
@@ -130,7 +131,7 @@
         n += 3
     for copy in loads + weights:
         copy.start()
-    for j in range(2):
+    for j in range(count):
         ds_[j][c, block(j, e), half:] = gate_ref[starts[j]:starts[j] + sizes[j], :]
 
     barrier = pltpu.get_barrier_semaphore()
@@ -154,8 +155,8 @@
         target = (first, up, down, last, e)[kind]
         view = bufs[t][j].at[core, block(j, blk)]
         return pltpu.make_async_remote_copy(
-            src_ref=view, dst_ref=view, send_sem=send.at[t * 2 + j, kind, blk],
-            recv_sem=recv.at[t * 2 + j, kind // 4, blk], **where(target, 1 - c if kind == 4 else c))
+            src_ref=view, dst_ref=view, send_sem=send.at[t * count + j, kind, blk],
+            recv_sem=recv.at[t * count + j, kind // 4, blk], **where(target, 1 - c if kind == 4 else c))
 
     def arrive(t, j, blk):
         gather_copy(t, j, 0, blk, c).wait_recv()
@@ -237,40 +238,41 @@
         @pl.loop(lo, hi)
         def _(i):
             cols = pl.ds(pl.multiple_of(i * 256, 256), 256)
-            pre[rows_of(j), cols] = lax.dot_general(
+            pre[:, cols] = lax.dot_general(
                 xs[j][0], wgu[0, cols, :], contract_last, preferred_element_type=f32
             ) + lax.dot_general(xs[j][1], wgu[1, cols, :], contract_last, preferred_element_type=f32)
 
-    def hidden_backward(j):
-        @pl.loop(0, sizes[j] * 16 // 256)
-        def _(i):
-            at = pl.ds(pl.multiple_of(i * 256, 256), 256)
-            hgrad[at, :] = lax.dot_general(
-                ds_[j][0, at, pl.ds(0, half)], wd[0], contract_last, preferred_element_type=f32
-            ) + lax.dot_general(ds_[j][1, at, pl.ds(0, half)], wd[1], contract_last, preferred_element_type=f32)
-
+    def hidden_grad(j):
+        hgrad[...] = lax.dot_general(
+            ds_[j][0, :, pl.ds(0, half)], wd[0], contract_last, preferred_element_type=f32
+        ) + lax.dot_general(ds_[j][1, :, pl.ds(0, half)], wd[1], contract_last, preferred_element_type=f32)
+
+    def elementwise(j):
         @pl.loop(0, sizes[j] * 16 // 64)
         def _(i):
-            there = pl.ds(pl.multiple_of(i * 64, 64), 64)
-            here = pl.ds(pl.multiple_of(starts[j] * 16 + i * 64, 64), 64)
+            here = pl.ds(pl.multiple_of(i * 64, 64), 64)
             lane = lax.broadcasted_iota(jnp.int32, (64, 128), 1)
-            pieces = ds_[j][0, there, pl.ds(half, 128)].astype(f32)
+            pieces = ds_[j][0, here, pl.ds(half, 128)].astype(f32)
             weight = jnp.sum(jnp.where(jnp.bitwise_and(lane, 15) == e, pieces, 0.0), axis=1, keepdims=True)
             gate_pre, up_pre = pre[here, pl.ds(0, hidden)], pre[here, pl.ds(hidden, hidden)]
             sigmoid = 1.0 / (1.0 + jnp.exp(-gate_pre))
             active = gate_pre * sigmoid
-            grad = hgrad[there, :] * weight
+            grad = hgrad[here, :] * weight
             hid[here, :] = (active * up_pre * weight).astype(jnp.bfloat16)
             act[here, pl.ds(hidden, hidden)] = (grad * active).astype(jnp.bfloat16)
             act[here, pl.ds(0, hidden)] = (
                 grad * up_pre * sigmoid * (1.0 + gate_pre * (1.0 - sigmoid))).astype(jnp.bfloat16)
 
+    def transposed(j):
+        act_t[:, rows_of(j)] = act[...].T
+        hid_t[:, rows_of(j)] = hid[...].T
+
     def row_backward(j, side, dest):
         @pl.loop(0, half // 512)
         def _(i):
             cols = pl.ds(pl.multiple_of(i * 512, 512), 512)
-            dest[j][:, cols] = jnp.dot(
-                act[rows_of(j), :], wgu[side, :, cols], preferred_element_type=f32).astype(jnp.bfloat16)
+            dest[:, cols] = jnp.dot(
+                act[...], wgu[side, :, cols], preferred_element_type=f32).astype(jnp.bfloat16)
 
     def plane_of(q):
         swapped = (0, 1, 3, 2)[q]
@@ -283,16 +285,19 @@
     def sibling_copy(j, zz):
         at = pl.ds(pl.multiple_of(zz * 4 * sizes[j], 16), 4 * sizes[j])
         return pltpu.make_async_remote_copy(
-            src_ref=sib_out[j].at[at], dst_ref=sib_in[j].at[at], send_sem=sib_send.at[j, zz],
+            src_ref=sib_out.at[at], dst_ref=sib_in[j].at[at], send_sem=sib_send.at[j, zz],
             recv_sem=sib_recv.at[j, zz], **where(e, 1 - c))
 
     def row_backward_out(j):
+        if j > 0:
+            for zz in planes:
+                sibling_copy(j - 1, zz).wait_send()
         row_backward(j, 1 - c, sib_out)
         for zz in planes:
             sibling_copy(j, zz).start()
 
     def row_backward_own(j):
-        row_backward(j, c, part)
+        row_backward(j, c, part[j])
 
     def add_rows(j, start, count, sources):
         dest = part[j]
@@ -313,7 +318,7 @@
             send_sem=last_send.at[j, slot], recv_sem=last_recv.at[j, slot], **where(last, c))
 
     def z_copy(j, way, zz, aa):
-        slot = way * 8 + zz * 2 + aa
+        slot = (zz + 1 - way) * 2 + aa
         return pltpu.make_async_remote_copy(
             src_ref=part[j].at[block(j, index(aa, b, zz))], dst_ref=from_z[j].at[slot],
             send_sem=z_send.at[j, slot], recv_sem=z_recv.at[j, slot], **where(down if way else up, c))
@@ -321,8 +326,9 @@
     def reduce_last(j, q):
         zz = planes[q]
         sibling_copy(j, zz).wait_recv()
-        add_rows(j, zz * 4 * sizes[j], 4 * sizes[j], [(sib_in[j], None, zz * 4 * sizes[j])])
         for aa in range(2):
+            start = index(aa, 1 - b, zz) * sizes[j]
+            add_rows(j, start, sizes[j], [(sib_in[j], None, start)])
             last_copy(j, zz, aa).start()
 
     def reduce_z(j, q):
@@ -330,7 +336,7 @@
         for aa in range(2):
             start = index(aa, b, zz) * sizes[j]
             last_copy(j, zz, aa).wait_recv()
-            add_rows(j, start, sizes[j], [(from_last[j], zz * 2 + aa, 0)])
+            add_rows(j, start, sizes[j], [(sib_in[j], None, start), (from_last[j], zz * 2 + aa, 0)])
             for way in range(2):
                 reached = (z > 0) if way == 0 else (z < 3)
                 ours = True if final else (zz > z if way == 0 else zz < z)
@@ -338,7 +344,7 @@
                 @pl.when(jnp.logical_and(reached, ours))
                 def _():
                     z_copy(j, way, zz, aa).wait_recv()
-                    add_rows(j, start, sizes[j], [(from_z[j], way * 8 + zz * 2 + aa, 0)])
+                    add_rows(j, start, sizes[j], [(from_z[j], (zz + 1 - way) * 2 + aa, 0)])
 
                 if not final:
                     pl.when(ours)(z_copy(j, way, zz, aa).start)
@@ -361,118 +367,115 @@
     outs = (gg_ref, gu_ref, gd_ref)
 
     def weight_copy(m, h):
-        held = wgu.at[h, pl.ds(m * hidden, hidden)] if m < 2 else wd.at[h]
+        held = acc.at[h, pl.ds(m * hidden, hidden)] if m < 2 else wd.at[h]
         return pltpu.make_async_copy(held, outs[m].at[0, :, pl.ds(h * half, half)], out_sem.at[m, h])
 
-    def weight_grad(m, h):
+    def weight_grad(m, h, chunks, more=False):
         lhs, rhs = (act_t, xs) if m < 2 else (hid_t, ds_)
-        base = m * hidden if m < 2 else 0
+        rows = pl.ds(m * hidden if m < 2 else 0, hidden)
+        dest = acc if m < 2 else wd
 
         @pl.loop(0, half // 512)
         def _(i):
             cols = pl.ds(pl.multiple_of(i * 512, 512), 512)
-            total = jnp.dot(
-                lhs[pl.ds(base, hidden), rows_of(0)], rhs[0][h, :, cols], preferred_element_type=f32
-            ) + jnp.dot(lhs[pl.ds(base, hidden), rows_of(1)], rhs[1][h, :, cols], preferred_element_type=f32)
-            if m < 2:
-                wgu[h, pl.ds(base, hidden), cols] = total.astype(jnp.bfloat16)
-            else:
-                wd[h, :, cols] = total.astype(jnp.bfloat16)
-
+            total = dest[h, rows, cols].astype(f32) if more else None
+            for j in chunks:
+                term = jnp.dot(lhs[rows, rows_of(j)], rhs[j][h, :, cols], preferred_element_type=f32)
+                total = term if total is None else total + term
+            dest[h, rows, cols] = total.astype(jnp.bfloat16)
+
+    def weight_done(m, h, chunks, more=False):
+        weight_grad(m, h, chunks, more)
         weight_copy(m, h).start()
 
-    X, G = 0, 1
-    own(X, 0)
-    first_step(X, 0)
-    z_step(X, 0, 1)
-    own(G, 0)
-    last_step(X, 0, 0)
-    z_step(X, 0, 2)
-    last_step(X, 0, 1)
-    z_step(X, 0, 3)
-    first_step(G, 0)
-    last_step(X, 0, 2)
-    z_step(G, 0, 1)
-    last_step(X, 0, 3)
-    last_step(G, 0, 0)
-    own(X, 1)
+    order = [(t, j) for j in range(count) for t in range(2)]
+
+    def stage(n, work):
+        tj = order[n]
+        following = order[n + 1] if n + 1 < len(order) else None
+        last_step(*tj, 0)
+        z_step(*tj, 2)
+        if following:
+            own(*following)
+        for do in work[0]:
+            do()
+        last_step(*tj, 1)
+        z_step(*tj, 3)
+        if following:
+            first_step(*following)
+        for do in work[1]:
+            do()
+        last_step(*tj, 2)
+        if following:
+            z_step(*following, 1)
+        for do in work[2]:
+            do()
+        last_step(*tj, 3)
+        for do in work[3]:
+            do()
+        sibling_step(*tj)
+
+    def call(f, *args):
+        return lambda: f(*args)
+
+    own(0, 0)
+    first_step(0, 0)
+    z_step(0, 0, 1)
+    stage(0, ((), (), (), ()))
     for copy in weights:
         copy.wait()
-    sibling_step(X, 0)
-    z_step(G, 0, 2)
-    forward(0, 0, 1)
-    last_step(G, 0, 1)
-    z_step(G, 0, 3)
-    first_step(X, 1)
-    own(G, 1)
-    forward(0, 1, 2)
-    last_step(G, 0, 2)
-    z_step(X, 1, 1)
-    forward(0, 2, 3)
-    last_step(G, 0, 3)
-    last_step(X, 1, 0)
-    sibling_step(G, 0)
-
-    hidden_backward(0)
-    z_step(X, 1, 2)
-    last_step(X, 1, 1)
-    first_step(G, 1)
-    row_backward_out(0)
-    z_step(X, 1, 3)
-    last_step(X, 1, 2)
-    z_step(G, 1, 1)
-    row_backward_own(0)
-    last_step(X, 1, 3)
-    last_step(G, 1, 0)
-    reduce_last(0, 0)
-    z_step(G, 1, 2)
-    reduce_last(0, 1)
-    last_step(G, 1, 1)
-    reduce_z(0, 0)
-    sibling_step(X, 1)
-    z_step(G, 1, 3)
-    reduce_last(0, 2)
-    reduce_z(0, 1)
-    last_step(G, 1, 2)
-    reduce_last(0, 3)
-    forward(1, 0, 3)
-    last_step(G, 1, 3)
-    reduce_z(0, 2)
-    sibling_step(G, 1)
-
-    hidden_backward(1)
-    row_backward_out(1)
-    row_backward_own(1)
-    reduce_last(1, 0)
-    reduce_last(1, 1)
-    reduce_z(0, 3)
-    first_copy(0).start()
-    reduce_last(1, 2)
-    reduce_z(1, 0)
-    reduce_last(1, 3)
-    act_t[...] = act[...].T
-    weight_grad(0, 0)
-    reduce_z(1, 1)
-    weight_grad(0, 1)
-    weight_grad(1, 0)
-    reduce_z(1, 2)
-    weight_grad(1, 1)
-    finish(0)
-    hid_t[...] = hid[...].T
+    stage(1, ([call(forward, 0, 0, 1)], [call(forward, 0, 1, 2)], [call(forward, 0, 2, 3)], ()))
+    for j in range(2):
+        stage(2 * j + 2, (
+            [call(hidden_grad, j), call(elementwise, j)],
+            [call(row_backward_out, j)],
+            [call(row_backward_own, j)],
+            ([call(reduce_z, j - 1, 3), call(first_copy(j - 1).start)] if j > 0 else [])
+            + [call(reduce_last, j, 0), call(reduce_last, j, 1), call(transposed, j)],
+        ))
+        stage(2 * j + 3, (
+            [call(forward, j + 1, 0, 1), call(reduce_last, j, 2), call(reduce_z, j, 0)],
+            [call(forward, j + 1, 1, 2), call(reduce_last, j, 3)],
+            [call(forward, j + 1, 2, 3), call(reduce_z, j, 1)],
+            [call(weight_grad, 0, 0, (0, 1)), call(reduce_z, j, 2), call(weight_grad, 0, 1, (0, 1))]
+            if j == 1 else [call(reduce_z, j, 2)],
+        ))
+
+    hidden_grad(2)
+    elementwise(2)
+    row_backward_out(2)
+    row_backward_own(2)
+    reduce_last(2, 0)
+    reduce_last(2, 1)
     reduce_z(1, 3)
     first_copy(1).start()
-    weight_grad(2, 0)
-    weight_grad(2, 1)
+    reduce_last(2, 2)
+    reduce_z(2, 0)
+    reduce_last(2, 3)
+    transposed(2)
+    weight_done(0, 0, (2,), True)
+    reduce_z(2, 1)
+    weight_done(0, 1, (2,), True)
+    weight_done(1, 0, (0, 1, 2))
+    reduce_z(2, 2)
+    weight_done(1, 1, (0, 1, 2))
+    finish(0)
     finish(1)
+    reduce_z(2, 3)
+    first_copy(2).start()
+    weight_done(2, 0, (0, 1, 2))
+    weight_done(2, 1, (0, 1, 2))
+    finish(2)
 
     for m in range(3):
         for h in range(2):
             weight_copy(m, h).wait()
-    for j in range(2):
+    for j in range(count):
         first_copy(j).wait_send()
         for q in range(4):
             zz = planes[q]
-            sibling_copy(j, zz).wait_send()
+            if j == count - 1:
+                sibling_copy(j, zz).wait_send()
             for aa in range(2):
                 last_copy(j, zz, aa).wait_send()
                 if q < 3:
@@ -487,7 +490,7 @@
     hidden = w_gate.shape[1]
     experts = lax.axis_size("expert")
     total = rows * experts
-    sizes = (rows // 48 * 32, rows // 48 * 16)
+    sizes = (rows // 3,) * 3
     chosen = expert_ids[:, :, None] == jnp.arange(experts, dtype=jnp.int32)[None, None, :]
     dense = jnp.sum(jnp.where(chosen, gate_values[:, :, None], 0.0), axis=1)
     high = lax.reduce_precision(dense, 8, 7)
@@ -501,7 +504,7 @@
     whole = tuple(size * experts for size in sizes)
 
     def chunks(*shape):
-        return [pltpu.VMEM(tuple(n[j] if isinstance(n, tuple) else n for n in shape), bf16) for j in range(2)]
+        return [pltpu.VMEM(tuple(n[j] if isinstance(n, tuple) else n for n in shape), bf16) for j in range(3)]
 
     return tuple(pl.pallas_call(
         functools.partial(merge_kernel, sizes),
@@ -518,33 +521,34 @@
             chunks(2, whole, half + 128),
             pltpu.VMEM((2, 2 * hidden, half), bf16),
             pltpu.VMEM((2, hidden, half), bf16),
-            pltpu.VMEM((total, 2 * hidden), f32),
+            pltpu.VMEM((whole[0], 2 * hidden), f32),
             pltpu.VMEM((whole[0], hidden), f32),
-            pltpu.VMEM((total, 2 * hidden), bf16),
-            pltpu.VMEM((total, hidden), bf16),
+            pltpu.VMEM((whole[0], 2 * hidden), bf16),
+            pltpu.VMEM((whole[0], hidden), bf16),
             pltpu.VMEM((2 * hidden, total), bf16),
             pltpu.VMEM((hidden, total), bf16),
             chunks(whole, half),
-            chunks(whole, half),
+            pltpu.VMEM((whole[0], half), bf16),
             chunks(whole, half),
             chunks(8, sizes, half),
-            chunks(16, sizes, half),
+            chunks(10, sizes, half),
             chunks(sizes, half),
-            dma((10,)),
-            dma((4, 5, 16)),
-            dma((4, 2, 16)),
-            dma((2, 4)),
-            dma((2, 4)),
-            dma((2, 8)),
-            dma((2, 8)),
-            dma((2, 16)),
-            dma((2, 16)),
-            dma((2,)),
-            dma((2,)),
+            pltpu.VMEM((2, 2 * hidden, half), bf16),
+            dma((12,)),
+            dma((6, 5, 16)),
+            dma((6, 2, 16)),
+            dma((3, 4)),
+            dma((3, 4)),
+            dma((3, 8)),
+            dma((3, 8)),
+            dma((3, 10)),
+            dma((3, 10)),
+            dma((3,)),
+            dma((3,)),
             dma((3, 2)),
         ],
         compiler_params=pltpu.CompilerParams(
-            collective_id=0, has_side_effects=True, vmem_limit_bytes=43 * 1024 * 1024),
+            collective_id=0, has_side_effects=True, vmem_limit_bytes=45 * 1024 * 1024),
         cost_estimate=pl.CostEstimate(
             flops=16 * total * hidden * 2 * half, bytes_accessed=24 * hidden * half, transcendentals=total * hidden),
     )(tokens, cotangent, gates, w_gate, w_up, w_down))

time: 122 us -> 134 us (1.098)
  Pallas kernels: 112 us -> 123 us
  local copies, waits for them, and re-layouts: 7.76 us -> 9.12 us
    pallas_call x1, Pallas kernels: 112 us -> 123 us  [on_device_tree(): pl.pallas_call(functools.partial(merge_kernel, sizes), out_shape=(jax.Sha...]
    unnamed x8 -> x10, local copies, waits for them, and re-layouts: 7.52 us -> 8.88 us
where the time goes in v3:
time: 134 us
  Pallas kernels  123 us (92%)
  local copies, waits for them, and re-layouts  9.12 us (7%)
    pallas_call x1, Pallas kernels, on_device_tree(): pl.pallas_call(functools.partial(merge_kernel, sizes), out_shape=(jax.Sha...  123 us
    unnamed x10, local copies, waits for them, and re-layouts  8.88 us

profile of v3, /device:TPU:0, one launch (start us, length us, event | category | flops | bytes accessed | tf_op | source)
XLA Modules:
  0.0 134.0 jit_solution(14730504426166062423)
XLA Ops:
  0.6 0.1 pad.3.clone
  0.7 0.7 select_reduce_fusion
  1.5 0.1 copy.16
  1.5 0.1 copy.15
  1.6 0.1 maximum_maximum_fusion.gate_ref
  1.7 0.0 copy-start
  1.7 0.9 copy-done
  2.6 0.0 copy-start.1
  2.6 0.9 copy-done.1
  3.6 123.4 %shard_map.102 = (bf16[48,2048]{1,0:T(8,128)(2,1)S(1)}, bf16[1,384,4096]{2,1,0:T(8,128)(2,1)S(1)}, bf16[1,384,4096]{2,1,0:T(8,128)(2,1)S(1)}, bf16[1,384,4096]{2,1,0:T(8,128)(2,1)}) custom-call(bf16[48,2048]{1,0:T(8,128)(2,1)S(1)} %copy-done, bf16[48,2048]{1,0:T(8,128)(2,1)S(1)} %copy-done.1, bf16[48,128]{1,0:T(8,128)(2,1)S(1)} %maximum_maximum_fusion.gate_ref, ...), custom_call_target="tpu_custom_call" | custom-call | flops 19327352832 | bytes 18874368 | tf_op jit(solution)/shard_map/pallas_call | solution.py:509
  127.0 0.7 copy.22
  127.7 1.7 %copy.23 = bf16[1,384,4096]{2,1,0:T(8,128)(2,1)} copy(bf16[1,384,4096]{2,1,0:T(8,128)(2,1)S(1)} %get-tuple-element.12) | data formatting | bytes 6291456
  129.4 0.0 copy-start.2
  129.4 1.7 %copy.24 = bf16[1,384,4096]{2,1,0:T(8,128)(2,1)} copy(bf16[1,384,4096]{2,1,0:T(8,128)(2,1)S(1)} %get-tuple-element.13) | data formatting | bytes 6291456
  131.0 1.4 %copy-done.2 = bf16[1,384,4096]{2,1,0:T(8,128)(2,1)S(1)} copy-done((bf16[1,384,4096]{2,1,0:T(8,128)(2,1)S(1)}, bf16[1,384,4096]{2,1,0:T(8,128)(2,1)}, u32[]{:S(2)}) %copy-start.2) | copy-done | bytes 3145752
  132.4 1.7 %copy.25 = bf16[1,384,4096]{2,1,0:T(8,128)(2,1)} copy(bf16[1,384,4096]{2,1,0:T(8,128)(2,1)S(1)} %copy-done.2) | data formatting | bytes 6291456
  (3 shorter events, 0.0 us)
Async XLA Ops:
  1.7 0.9 copy-start
  2.6 0.9 copy-start.1
  129.4 3.0 %copy-start.2 = (bf16[1,384,4096]{2,1,0:T(8,128)(2,1)S(1)}, bf16[1,384,4096]{2,1,0:T(8,128)(2,1)}, u32[]{:S(2)}) copy-start(bf16[1,384,4096]{2,1,0:T(8,128)(2,1)} %get-tuple-element.14) | copy-start | bytes 9437188

commit v4 on v2

--- a/solution.py
+++ b/solution.py
@@ -91,7 +91,7 @@
     sizes, tok_ref, cot_ref, gate_ref, wg_ref, wu_ref, wd_ref,
     out_ref, gg_ref, gu_ref, gd_ref,
     xs, ds_, wgu, wd, pre, hgrad, act, hid, act_t, hid_t, part, sib_out, sib_in, from_last, from_z, from_first,
-    load_sem, send, recv, sib_send, sib_recv, last_send, last_recv, z_send, z_recv, first_send, first_recv, out_sem,
+    load_sem, send, recv, across_send, across_recv, sib_send, sib_recv, last_send, last_recv, z_send, z_recv, first_send, first_recv, out_sem,
 ):
     half = tok_ref.shape[1]
     hidden = wg_ref.shape[1]
@@ -150,19 +150,26 @@
     for copy in loads:
         copy.wait()
 
-    def gather_copy(t, j, kind, blk, core):
-        target = (first, up, down, last, e)[kind]
-        view = bufs[t][j].at[core, block(j, blk)]
+    def gather_copy(t, j, kind, blk):
+        view = bufs[t][j].at[c, block(j, blk)]
         return pltpu.make_async_remote_copy(
-            src_ref=view, dst_ref=view, send_sem=send.at[t * 2 + j, kind, blk],
-            recv_sem=recv.at[t * 2 + j, kind // 4, blk], **where(target, 1 - c if kind == 4 else c))
+            src_ref=view, dst_ref=view, send_sem=send.at[t * 2 + j, kind, 0 if kind == 3 else blk],
+            recv_sem=recv.at[t * 2 + j, blk], **where((first, up, down, last)[kind], c))
+
+    def across(t, j, view):
+        return pltpu.make_async_remote_copy(
+            src_ref=view, dst_ref=view, send_sem=across_send.at[t * 2 + j],
+            recv_sem=across_recv.at[t * 2 + j], **where(e, 1 - c))
+
+    def plane(t, j, zz):
+        across(t, j, bufs[t][j].at[c, pl.ds(pl.multiple_of(zz * 4 * sizes[j], 16), 4 * sizes[j])]).start()
 
     def arrive(t, j, blk):
-        gather_copy(t, j, 0, blk, c).wait_recv()
+        gather_copy(t, j, 0, blk).wait_recv()
 
     def each(t, j, blk, kinds, verb):
         for kind in kinds:
-            do = getattr(gather_copy(t, j, kind, blk, c), verb)
+            do = getattr(gather_copy(t, j, kind, blk), verb)
             if kind == 1:
                 pl.when(z < 3)(do)
             elif kind == 2:
@@ -171,12 +178,12 @@
                 do()
 
     def own(t, j):
-        each(t, j, e, (0, 1, 2, 3, 4), "start")
+        each(t, j, e, (0, 1, 2, 3), "start")
 
     def first_step(t, j):
         blk = index(1 - a, b, z)
         arrive(t, j, blk)
-        each(t, j, blk, (1, 2, 3, 4), "start")
+        each(t, j, blk, (1, 2, 3), "start")
 
     def z_step(t, j, k):
         for aa in (a, 1 - a):
@@ -184,49 +191,41 @@
             def _():
                 blk = index(aa, b, z - k)
                 arrive(t, j, blk)
-                each(t, j, blk, (1, 3, 4), "start")
+                each(t, j, blk, (1, 3), "start")
 
             @pl.when(z + k <= 3)
             def _():
                 blk = index(aa, b, z + k)
                 arrive(t, j, blk)
-                each(t, j, blk, (2, 3, 4), "start")
+                each(t, j, blk, (2, 3), "start")
 
     def last_step(t, j, k):
-        def over(blk):
-            arrive(t, j, blk)
-            each(t, j, blk, (4,), "start")
-
-        for aa in (a, 1 - a):
-            if k == 0:
-                over(index(aa, 1 - b, z))
-                continue
-
-            @pl.when(z >= k)
-            def _():
-                over(index(aa, 1 - b, z - k))
-
-            @pl.when(z + k <= 3)
-            def _():
-                over(index(aa, 1 - b, z + k))
+        def over(zz):
+            for aa in (a, 1 - a):
+                arrive(t, j, index(aa, 1 - b, zz))
+            plane(t, j, zz)
+
+        if k == 0:
+            over(z)
+        else:
+            pl.when(z >= k)(lambda: over(z - k))
+            pl.when(z + k <= 3)(lambda: over(z + k))
 
     def sibling_step(t, j):
-        @pl.loop(0, 16)
-        def _(blk):
-            gather_copy(t, j, 4, blk, 1 - c).wait_recv()
+        across(t, j, bufs[t][j].at[1 - c]).wait_recv()
 
     def gather_sent(t, j):
-        each(t, j, e, (0, 1, 2, 3, 4), "wait_send")
-        each(t, j, index(1 - a, b, z), (1, 2, 3, 4), "wait_send")
+        each(t, j, e, (0, 1, 2), "wait_send")
+        each(t, j, index(1 - a, b, z), (1, 2), "wait_send")
         for k in range(1, 4):
             for aa in (a, 1 - a):
-                pl.when(z >= k)(lambda: each(t, j, index(aa, b, z - k), (1, 3, 4), "wait_send"))
-                pl.when(z + k <= 3)(lambda: each(t, j, index(aa, b, z + k), (2, 3, 4), "wait_send"))
-
-        @pl.loop(0, 4)
-        def _(zz):
-            for aa in range(2):
-                gather_copy(t, j, 4, index(aa, 1 - b, zz), c).wait_send()
+                pl.when(z >= k)(lambda: each(t, j, index(aa, b, z - k), (1,), "wait_send"))
+                pl.when(z + k <= 3)(lambda: each(t, j, index(aa, b, z + k), (2,), "wait_send"))
+        eight = bufs[t][j].at[c, pl.ds(0, 8 * sizes[j])]
+        pltpu.make_async_remote_copy(
+            src_ref=eight, dst_ref=eight, send_sem=send.at[t * 2 + j, 3, 0], recv_sem=recv.at[t * 2 + j, 0],
+            **where(last, c)).wait_send()
+        across(t, j, bufs[t][j].at[c]).wait_send()
 
     contract_last = (((1,), (1,)), ((), ()))
 
@@ -237,7 +236,7 @@
         @pl.loop(lo, hi)
         def _(i):
             cols = pl.ds(pl.multiple_of(i * 256, 256), 256)
-            pre[rows_of(j), cols] = lax.dot_general(
+            pre[pl.ds(0, sizes[j] * 16), cols] = lax.dot_general(
                 xs[j][0], wgu[0, cols, :], contract_last, preferred_element_type=f32
             ) + lax.dot_general(xs[j][1], wgu[1, cols, :], contract_last, preferred_element_type=f32)
 
@@ -256,7 +255,7 @@
             lane = lax.broadcasted_iota(jnp.int32, (64, 128), 1)
             pieces = ds_[j][0, there, pl.ds(half, 128)].astype(f32)
             weight = jnp.sum(jnp.where(jnp.bitwise_and(lane, 15) == e, pieces, 0.0), axis=1, keepdims=True)
-            gate_pre, up_pre = pre[here, pl.ds(0, hidden)], pre[here, pl.ds(hidden, hidden)]
+            gate_pre, up_pre = pre[there, pl.ds(0, hidden)], pre[there, pl.ds(hidden, hidden)]
             sigmoid = 1.0 / (1.0 + jnp.exp(-gate_pre))
             active = gate_pre * sigmoid
             grad = hgrad[there, :] * weight
@@ -313,7 +312,7 @@
             send_sem=last_send.at[j, slot], recv_sem=last_recv.at[j, slot], **where(last, c))
 
     def z_copy(j, way, zz, aa):
-        slot = way * 8 + zz * 2 + aa
+        slot = (zz + 1 - way) * 2 + aa
         return pltpu.make_async_remote_copy(
             src_ref=part[j].at[block(j, index(aa, b, zz))], dst_ref=from_z[j].at[slot],
             send_sem=z_send.at[j, slot], recv_sem=z_recv.at[j, slot], **where(down if way else up, c))
@@ -321,8 +320,9 @@
     def reduce_last(j, q):
         zz = planes[q]
         sibling_copy(j, zz).wait_recv()
-        add_rows(j, zz * 4 * sizes[j], 4 * sizes[j], [(sib_in[j], None, zz * 4 * sizes[j])])
         for aa in range(2):
+            start = index(aa, 1 - b, zz) * sizes[j]
+            add_rows(j, start, sizes[j], [(sib_in[j], None, start)])
             last_copy(j, zz, aa).start()
 
     def reduce_z(j, q):
@@ -330,7 +330,7 @@
         for aa in range(2):
             start = index(aa, b, zz) * sizes[j]
             last_copy(j, zz, aa).wait_recv()
-            add_rows(j, start, sizes[j], [(from_last[j], zz * 2 + aa, 0)])
+            add_rows(j, start, sizes[j], [(sib_in[j], None, start), (from_last[j], zz * 2 + aa, 0)])
             for way in range(2):
                 reached = (z > 0) if way == 0 else (z < 3)
                 ours = True if final else (zz > z if way == 0 else zz < z)
@@ -338,7 +338,7 @@
                 @pl.when(jnp.logical_and(reached, ours))
                 def _():
                     z_copy(j, way, zz, aa).wait_recv()
-                    add_rows(j, start, sizes[j], [(from_z[j], way * 8 + zz * 2 + aa, 0)])
+                    add_rows(j, start, sizes[j], [(from_z[j], (zz + 1 - way) * 2 + aa, 0)])
 
                 if not final:
                     pl.when(ours)(z_copy(j, way, zz, aa).start)
@@ -391,15 +391,15 @@
     last_step(X, 0, 1)
     z_step(X, 0, 3)
     first_step(G, 0)
+    own(X, 1)
     last_step(X, 0, 2)
     z_step(G, 0, 1)
     last_step(X, 0, 3)
-    last_step(G, 0, 0)
-    own(X, 1)
     for copy in weights:
         copy.wait()
+    last_step(G, 0, 0)
+    z_step(G, 0, 2)
     sibling_step(X, 0)
-    z_step(G, 0, 2)
     forward(0, 0, 1)
     last_step(G, 0, 1)
     z_step(G, 0, 3)
@@ -425,19 +425,23 @@
     last_step(X, 1, 3)
     last_step(G, 1, 0)
     reduce_last(0, 0)
+    reduce_last(0, 1)
     z_step(G, 1, 2)
-    reduce_last(0, 1)
+    reduce_z(0, 0)
+    reduce_last(0, 2)
+    sibling_step(X, 1)
     last_step(G, 1, 1)
-    reduce_z(0, 0)
-    sibling_step(X, 1)
+    forward(1, 0, 1)
     z_step(G, 1, 3)
-    reduce_last(0, 2)
     reduce_z(0, 1)
+    reduce_last(0, 3)
+    forward(1, 1, 2)
     last_step(G, 1, 2)
-    reduce_last(0, 3)
-    forward(1, 0, 3)
+    reduce_z(0, 2)
+    forward(1, 2, 3)
     last_step(G, 1, 3)
-    reduce_z(0, 2)
+    reduce_z(0, 3)
+    first_copy(0).start()
     sibling_step(G, 1)
 
     hidden_backward(1)
@@ -445,8 +449,6 @@
     row_backward_own(1)
     reduce_last(1, 0)
     reduce_last(1, 1)
-    reduce_z(0, 3)
-    first_copy(0).start()
     reduce_last(1, 2)
     reduce_z(1, 0)
     reduce_last(1, 3)
@@ -487,7 +489,7 @@
     hidden = w_gate.shape[1]
     experts = lax.axis_size("expert")
     total = rows * experts
-    sizes = (rows // 48 * 32, rows // 48 * 16)
+    sizes = (rows // 48 * 16, rows // 48 * 32)
     chosen = expert_ids[:, :, None] == jnp.arange(experts, dtype=jnp.int32)[None, None, :]
     dense = jnp.sum(jnp.where(chosen, gate_values[:, :, None], 0.0), axis=1)
     high = lax.reduce_precision(dense, 8, 7)
@@ -518,8 +520,8 @@
             chunks(2, whole, half + 128),
             pltpu.VMEM((2, 2 * hidden, half), bf16),
             pltpu.VMEM((2, hidden, half), bf16),
-            pltpu.VMEM((total, 2 * hidden), f32),
-            pltpu.VMEM((whole[0], hidden), f32),
+            pltpu.VMEM((whole[1], 2 * hidden), f32),
+            pltpu.VMEM((whole[1], hidden), f32),
             pltpu.VMEM((total, 2 * hidden), bf16),
             pltpu.VMEM((total, hidden), bf16),
             pltpu.VMEM((2 * hidden, total), bf16),
@@ -528,17 +530,19 @@
             chunks(whole, half),
             chunks(whole, half),
             chunks(8, sizes, half),
-            chunks(16, sizes, half),
+            chunks(10, sizes, half),
             chunks(sizes, half),
             dma((10,)),
-            dma((4, 5, 16)),
-            dma((4, 2, 16)),
+            dma((4, 4, 16)),
+            dma((4, 16)),
+            dma((4,)),
+            dma((4,)),
             dma((2, 4)),
             dma((2, 4)),
             dma((2, 8)),
             dma((2, 8)),
-            dma((2, 16)),
-            dma((2, 16)),
+            dma((2, 10)),
+            dma((2, 10)),
             dma((2,)),
             dma((2,)),
             dma((3, 2)),

time: 122 us -> 124 us (1.016)
  Pallas kernels: 112 us -> 115 us
    pallas_call x1, Pallas kernels: 112 us -> 115 us  [on_device_tree(): pl.pallas_call(functools.partial(merge_kernel, sizes), out_shape=(jax.Sha...]
where the time goes in v4:
time: 124 us
  Pallas kernels  115 us (93%)
  local copies, waits for them, and re-layouts  7.76 us (6%)
    pallas_call x1, Pallas kernels, on_device_tree(): pl.pallas_call(functools.partial(merge_kernel, sizes), out_shape=(jax.Sha...  115 us
    unnamed x8, local copies, waits for them, and re-layouts  7.52 us

profile of v4, /device:TPU:0, one launch (start us, length us, event | category | flops | bytes accessed | tf_op | source)
XLA Modules:
  0.0 124.1 jit_solution(13693616789799561820)
XLA Ops:
  0.6 0.1 pad.3.clone
  0.7 0.7 select_reduce_fusion
  1.5 0.1 copy.16
  1.5 0.1 copy.15
  1.6 0.1 maximum_maximum_fusion.gate_ref
  1.7 0.0 copy-start
  1.7 0.9 copy-done
  2.6 0.0 copy-start.1
  2.6 0.9 copy-done.1
  3.6 114.9 %shard_map.102 = (bf16[48,2048]{1,0:T(8,128)(2,1)S(1)}, bf16[1,384,4096]{2,1,0:T(8,128)(2,1)S(1)}, bf16[1,384,4096]{2,1,0:T(8,128)(2,1)S(1)}, bf16[1,384,4096]{2,1,0:T(8,128)(2,1)S(1)}) custom-call(bf16[48,2048]{1,0:T(8,128)(2,1)S(1)} %copy-done, bf16[48,2048]{1,0:T(8,128)(2,1)S(1)} %copy-done.1, bf16[48,128]{1,0:T(8,128)(2,1)S(1)} %maximum_maximum_fusion.gate_ref, ...), custom_call_target="tpu_custom_call" | custom-call | flops 19327352832 | bytes 18874368 | tf_op jit(solution)/shard_map/pallas_call | solution.py:508
  118.4 0.7 copy.22
  119.1 1.7 %copy.23 = bf16[1,384,4096]{2,1,0:T(8,128)(2,1)} copy(bf16[1,384,4096]{2,1,0:T(8,128)(2,1)S(1)} %get-tuple-element.12) | data formatting | bytes 6291456
  120.8 1.7 %copy.24 = bf16[1,384,4096]{2,1,0:T(8,128)(2,1)} copy(bf16[1,384,4096]{2,1,0:T(8,128)(2,1)S(1)} %get-tuple-element.13) | data formatting | bytes 6291456
  122.5 1.7 %copy.25 = bf16[1,384,4096]{2,1,0:T(8,128)(2,1)} copy(bf16[1,384,4096]{2,1,0:T(8,128)(2,1)S(1)} %get-tuple-element.14) | data formatting | bytes 6291456
  (3 shorter events, 0.0 us)
Async XLA Ops:
  1.7 0.9 copy-start
  2.6 0.9 copy-start.1

commit v5 on v4

--- a/solution.py
+++ b/solution.py
@@ -264,6 +264,10 @@
             act[here, pl.ds(0, hidden)] = (
                 grad * up_pre * sigmoid * (1.0 + gate_pre * (1.0 - sigmoid))).astype(jnp.bfloat16)
 
+    def transposed(j):
+        act_t[:, rows_of(j)] = act[rows_of(j), :].T
+        hid_t[:, rows_of(j)] = hid[rows_of(j), :].T
+
     def row_backward(j, side, dest):
         @pl.loop(0, half // 512)
         def _(i):
@@ -391,13 +395,13 @@
     last_step(X, 0, 1)
     z_step(X, 0, 3)
     first_step(G, 0)
-    own(X, 1)
     last_step(X, 0, 2)
     z_step(G, 0, 1)
     last_step(X, 0, 3)
+    last_step(G, 0, 0)
+    own(X, 1)
     for copy in weights:
         copy.wait()
-    last_step(G, 0, 0)
     z_step(G, 0, 2)
     sibling_step(X, 0)
     forward(0, 0, 1)
@@ -425,44 +429,42 @@
     last_step(X, 1, 3)
     last_step(G, 1, 0)
     reduce_last(0, 0)
+    z_step(G, 1, 2)
     reduce_last(0, 1)
-    z_step(G, 1, 2)
+    last_step(G, 1, 1)
     reduce_z(0, 0)
+    sibling_step(X, 1)
+    z_step(G, 1, 3)
     reduce_last(0, 2)
-    sibling_step(X, 1)
-    last_step(G, 1, 1)
-    forward(1, 0, 1)
-    z_step(G, 1, 3)
     reduce_z(0, 1)
+    last_step(G, 1, 2)
     reduce_last(0, 3)
-    forward(1, 1, 2)
-    last_step(G, 1, 2)
+    forward(1, 0, 3)
+    last_step(G, 1, 3)
     reduce_z(0, 2)
-    forward(1, 2, 3)
-    last_step(G, 1, 3)
-    reduce_z(0, 3)
-    first_copy(0).start()
+    transposed(0)
     sibling_step(G, 1)
 
     hidden_backward(1)
     row_backward_out(1)
     row_backward_own(1)
+    reduce_z(0, 3)
+    first_copy(0).start()
     reduce_last(1, 0)
     reduce_last(1, 1)
     reduce_last(1, 2)
     reduce_z(1, 0)
     reduce_last(1, 3)
-    act_t[...] = act[...].T
+    transposed(1)
     weight_grad(0, 0)
     reduce_z(1, 1)
     weight_grad(0, 1)
+    reduce_z(1, 2)
     weight_grad(1, 0)
-    reduce_z(1, 2)
-    weight_grad(1, 1)
     finish(0)
-    hid_t[...] = hid[...].T
     reduce_z(1, 3)
     first_copy(1).start()
+    weight_grad(1, 1)
     weight_grad(2, 0)
     weight_grad(2, 1)
     finish(1)
@@ -489,7 +491,7 @@
     hidden = w_gate.shape[1]
     experts = lax.axis_size("expert")
     total = rows * experts
-    sizes = (rows // 48 * 16, rows // 48 * 32)
+    sizes = (rows // 48 * 32, rows // 48 * 16)
     chosen = expert_ids[:, :, None] == jnp.arange(experts, dtype=jnp.int32)[None, None, :]
     dense = jnp.sum(jnp.where(chosen, gate_values[:, :, None], 0.0), axis=1)
     high = lax.reduce_precision(dense, 8, 7)
@@ -520,8 +522,8 @@
             chunks(2, whole, half + 128),
             pltpu.VMEM((2, 2 * hidden, half), bf16),
             pltpu.VMEM((2, hidden, half), bf16),
-            pltpu.VMEM((whole[1], 2 * hidden), f32),
-            pltpu.VMEM((whole[1], hidden), f32),
+            pltpu.VMEM((whole[0], 2 * hidden), f32),
+            pltpu.VMEM((whole[0], hidden), f32),
             pltpu.VMEM((total, 2 * hidden), bf16),
             pltpu.VMEM((total, hidden), bf16),
             pltpu.VMEM((2 * hidden, total), bf16),

time: 124 us -> 123 us (level)
    pallas_call x1, Pallas kernels: 115 us -> 114 us  [on_device_tree(): pl.pallas_call(functools.partial(merge_kernel, sizes), out_shape=(jax.Sha...]
where the time goes in v5:
time: 123 us
  Pallas kernels  114 us (93%)
  local copies, waits for them, and re-layouts  7.76 us (6%)
    pallas_call x1, Pallas kernels, on_device_tree(): pl.pallas_call(functools.partial(merge_kernel, sizes), out_shape=(jax.Sha...  114 us
    unnamed x8, local copies, waits for them, and re-layouts  7.52 us

profile of v5, /device:TPU:0, one launch (start us, length us, event | category | flops | bytes accessed | tf_op | source)
XLA Modules:
  0.0 122.8 jit_solution(5242043524732464424)
XLA Ops:
  0.6 0.1 pad.3.clone
  0.7 0.7 select_reduce_fusion
  1.5 0.1 copy.16
  1.5 0.1 copy.15
  1.6 0.1 maximum_maximum_fusion.gate_ref
  1.7 0.0 copy-start
  1.7 0.9 copy-done
  2.6 0.0 copy-start.1
  2.6 0.9 copy-done.1
  3.6 113.5 %shard_map.102 = (bf16[48,2048]{1,0:T(8,128)(2,1)S(1)}, bf16[1,384,4096]{2,1,0:T(8,128)(2,1)S(1)}, bf16[1,384,4096]{2,1,0:T(8,128)(2,1)S(1)}, bf16[1,384,4096]{2,1,0:T(8,128)(2,1)S(1)}) custom-call(bf16[48,2048]{1,0:T(8,128)(2,1)S(1)} %copy-done, bf16[48,2048]{1,0:T(8,128)(2,1)S(1)} %copy-done.1, bf16[48,128]{1,0:T(8,128)(2,1)S(1)} %maximum_maximum_fusion.gate_ref, ...), custom_call_target="tpu_custom_call" | custom-call | flops 19327352832 | bytes 18874368 | tf_op jit(solution)/shard_map/pallas_call | solution.py:510
  117.1 0.7 copy.22
  117.8 1.7 %copy.23 = bf16[1,384,4096]{2,1,0:T(8,128)(2,1)} copy(bf16[1,384,4096]{2,1,0:T(8,128)(2,1)S(1)} %get-tuple-element.12) | data formatting | bytes 6291456
  119.4 1.7 %copy.24 = bf16[1,384,4096]{2,1,0:T(8,128)(2,1)} copy(bf16[1,384,4096]{2,1,0:T(8,128)(2,1)S(1)} %get-tuple-element.13) | data formatting | bytes 6291456
  121.1 1.7 %copy.25 = bf16[1,384,4096]{2,1,0:T(8,128)(2,1)} copy(bf16[1,384,4096]{2,1,0:T(8,128)(2,1)S(1)} %get-tuple-element.14) | data formatting | bytes 6291456
  (3 shorter events, 0.0 us)
Async XLA Ops:
  1.7 0.9 copy-start
  2.6 0.9 copy-start.1
